TPU v7x, 32 devices: a whole 2x2x4 slice. The times are simulated.
32 devices in a mesh: groups: 2 (over y), tile: 16 (over z, x, core).
Axes of the slice: x: 2, y: 2, z: 4, core: 2. Of those that a mesh axis runs over, the one named last changes fastest.
Arguments:
- object_slices: float32 [4096, 2, 2, 256], P(('groups', 'tile')), parts along dimension 0, may hold values from -4 to 4
- probe_field: float32 [256, 2, 2, 128], P(('groups', 'tile')), parts along dimension 0, may hold values from -2.5 to 2.5
- patterns: float32 [512, 128, 128], P(('groups', 'tile')), parts along dimension 0, may hold values from 0 to 2
- row_offsets: int32 [512], P(('groups', 'tile')), parts along dimension 0, may hold values from 0 to 127
- col_offsets: int32 [512], P(('groups', 'tile')), parts along dimension 0, may hold values from 0 to 128
- counts: int32 [32], P(('groups', 'tile')), parts along dimension 0, may hold values from 1 to 16, as said below
Outputs:
- object_grad: float32 [4096, 2, 2, 256], P(('groups', 'tile')), parts along dimension 0
- probe_grad: float32 [256, 2, 2, 128], P(('groups', 'tile')), parts along dimension 0
There are 2 independent parts, one for each index of `groups`. A program takes and returns all parts, laid end to end along the dimension named above; each array names one. Nothing has to cross between parts.
Inputs may be any that keep to these rules, and one draw needn't show every extreme that they name: `counts`: each tile has 1 to 16 live slots, and one tile of every draw has 16.
All inputs are finite; a program needn't handle non-finite values.
Results may differ from a plain program's by a relative error of at most 0.0003.
Values sent between devices are 32-bit elements; how exact they have to be, the bound alone decides.
No kernel may reach another device: no remote copies, remote signals or barrier semaphores. Data moves between devices by JAX's collectives and lax.ppermute only.
A program may use at most 64 MiB of HBM per device.

v0:
```python
import math

import jax
import jax.numpy as jnp
import numpy as np
from jax import lax
from jax.experimental import pallas as pl
from jax.experimental.pallas import tpu as pltpu
from jax.sharding import PartitionSpec as P

GROUP_DEV = 16
KAPPA = 4.0
MODES = 2
SLICES = 2
HALVES = 2
AHEAD = (0, 8, 4, 12, 2, 10, 6, 14)


def factors(extent):
    counter = np.arange(extent)
    half = extent // 2
    dft = np.exp(-2j * np.pi * (counter[:, None] * counter[None, :] % extent) / extent) / math.sqrt(extent)
    freq = ((counter + extent // 2) % extent - extent // 2) / extent
    prop = np.conj(dft) @ (np.exp(-1j * np.pi * KAPPA * freq**2)[:, None] * dft)
    whole = [part for matrix in (dft, prop) for part in (matrix.real, matrix.imag)]
    same, cross = prop[:half, :half], prop[:half, half:]
    even, odd = dft[0::2, :half], dft[1::2, :half]
    halves = [even, odd, np.conj(even.T), np.conj(odd.T),
              (same + cross) / 2, (same - cross) / 2, np.conj(same + cross) / 2, np.conj(same - cross) / 2]
    halves = [np.block([[m.real, -m.imag], [m.imag, m.real]]) for m in halves]
    return np.stack(whole + halves).astype(np.float32)


def split(value):
    high = value.astype(jnp.bfloat16)
    low = (value - high.astype(jnp.float32)).astype(jnp.bfloat16)
    return high, low


def prepare(own_ref, patterns_ref, factors_ref, planes_out, patterns_out, mats_out, half_out, own, parts, sems):
    copies = [pltpu.make_async_copy(source, target, sems.at[i]) for i, (source, target) in enumerate(
        ((factors_ref, parts), (own_ref, own), (patterns_ref, patterns_out)))]
    for copy in copies:
        copy.start()
    copies[0].wait()
    extent = parts.shape[1]
    for kind in range(2):
        real, imag = split(parts[2 * kind]), split(parts[2 * kind + 1])
        for conj in range(2):
            for k in range(2):
                mat = 4 * kind + 2 * conj + k
                upper, lower = (-imag[k], imag[k]) if conj else (imag[k], -imag[k])
                mats_out[mat, :extent, :extent] = real[k]
                mats_out[mat, :extent, extent:] = upper
                mats_out[mat, extent:, :extent] = lower
                mats_out[mat, extent:, extent:] = real[k]
    for k in range(half_out.shape[0]):
        high, low = split(parts[4 + k])
        half_out[k, :extent, :extent] = high
        half_out[k, :extent, extent:] = high
        half_out[k, extent:, :extent] = low
        half_out[k, extent:, extent:] = low
    copies[1].wait()
    rows = planes_out.shape[1]
    for layer in range(SLICES):
        for half in range(HALVES):
            for part in range(2):
                source = (layer * HALVES + half) * 2 + part
                plane = (layer * 2 + part) * HALVES + half
                planes_out[plane] = own[pl.ds(source, rows, stride=8), :]
    copies[2].wait()


def times(a, b):
    return [a[0] * b[0] - a[1] * b[1], a[0] * b[1] + a[1] * b[0]]


def conj_times(a, b):
    return [a[0] * b[0] + a[1] * b[1], a[0] * b[1] - a[1] * b[0]]


def add(a, b):
    return [a[0] + b[0], a[1] + b[1]]


def member_rows(member, order, share):
    return pl.ds(pl.multiple_of(lax.bitwise_xor(member, order) * share, share), share)


def place(probe_ref, keep_out, send_out):
    lanes, extent = probe_ref.shape[:2]
    share = extent // GROUP_DEV
    member = lax.rem(lax.axis_index("tile"), GROUP_DEV)
    for odd, ref in enumerate((keep_out, send_out)):
        for block in range(GROUP_DEV // 2):
            there = lax.bitwise_xor(lax.rem(member + block // 2 * 4, GROUP_DEV), 2 * (block % 2) + odd)
            for k in range(lanes):
                rows = pl.ds(block * share * lanes + k, share, stride=lanes)
                ref[rows, :] = probe_ref[k, pl.ds(pl.multiple_of(there * share, share), share), :]


def kernel(scalars_ref, own_ref, low_ref, high_ref, near_ref, far_ref, patterns_ref, mats_ref,
           half_ref, own_out, next_out, probe_acc, obj, acc, probe):
    most, extent = patterns_ref.shape[:2]
    share = extent // GROUP_DEV
    member = lax.rem(lax.axis_index("tile"), GROUP_DEV)
    tile_rows = own_ref.shape[1]
    middle = extent // 2
    lanes = 2 * MODES
    modes = range(MODES)

    for layer in range(SLICES):
        for half in range(HALVES):
            for part in range(2):
                source = (layer * HALVES + half) * 2 + part
                plane = (layer * 2 + part) * HALVES + half
                obj[plane, :tile_rows] = own_ref[plane]
                obj[plane, tile_rows:tile_rows + middle] = low_ref[pl.ds(source, middle, stride=8), :]
                obj[plane, tile_rows + middle:] = high_ref[pl.ds(source, extent - middle, stride=8), :]
    for odd, ref in enumerate((near_ref, far_ref)):
        for block, order in enumerate(AHEAD):
            for k in range(lanes):
                rows = pl.ds(block * share * lanes + k, share, stride=lanes)
                probe[k, member_rows(member, order + odd, share), :] = ref[rows, :]
    acc[...] = jnp.zeros(acc.shape, jnp.float32)
    probe_acc[...] = jnp.zeros(probe_acc.shape, jnp.float32)

    def right(fields, kind, conj):
        high_m, low_m = mats_ref[4 * kind + 2 * conj], mats_ref[4 * kind + 2 * conj + 1]
        rows = jnp.concatenate([jnp.concatenate(f[m], axis=1) for f in fields for m in modes], axis=0)
        high, low = split(rows)
        out = jnp.dot(jnp.concatenate([high, low, high], axis=1), jnp.concatenate([high_m, high_m, low_m], axis=0),
                      preferred_element_type=jnp.float32)
        return [[[out[(i * MODES + m) * extent:(i * MODES + m + 1) * extent, c * extent:(c + 1) * extent]
                  for c in range(2)] for m in modes] for i in range(len(fields))]

    def left(fields, kind, conj):
        middle = extent // 2
        cols = [jnp.concatenate([f[m][c] for f in fields for m in modes], axis=1) for c in range(2)]
        upper, lower = [c[:middle] for c in cols], [c[middle:] for c in cols]
        if kind == 1 or not conj:
            upper, lower = add(upper, lower), [u - v for u, v in zip(upper, lower)]
        halves = []
        for k, pieces in enumerate((upper, lower)):
            high, low = split(jnp.concatenate(pieces, axis=0))
            out = jnp.dot(half_ref[4 * kind + 2 * conj + k], jnp.concatenate([high, low], axis=0),
                          preferred_element_type=jnp.float32)
            out = out[:extent] + out[extent:]
            halves.append([out[:middle], out[middle:]])
        upper, lower = halves
        if kind == 1 or conj:
            upper, lower = add(upper, lower), [u - v for u, v in zip(upper, lower)]
        out = [jnp.concatenate([upper[c], lower[c]], axis=0) for c in range(2)]
        return [[[out[c][:, (i * MODES + m) * extent:(i * MODES + m + 1) * extent] for c in range(2)]
                 for m in modes] for i in range(len(fields))]

    lane = lax.broadcasted_iota(jnp.int32, (extent, extent), 1)

    def window(slot):
        r, c = scalars_ref[slot], scalars_ref[most + slot]
        shift = lax.rem(extent - c, extent)
        layers = []
        for layer in range(SLICES):
            parts = []
            for part in range(2):
                plane = (layer * 2 + part) * HALVES
                joined = jnp.where(lane >= c, obj[plane, pl.ds(r, extent), :], obj[plane + 1, pl.ds(r, extent), :])
                parts.append(pltpu.roll(joined, shift, 1))
            layers.append(parts)
        return layers

    def deposit(slot, layer, grad):
        r, c = scalars_ref[slot], scalars_ref[most + slot]
        for part in range(2):
            plane = (layer * 2 + part) * HALVES
            rolled = pltpu.roll(grad[part], lax.rem(c, extent), 1)
            acc[plane, pl.ds(r, extent), :] += jnp.where(lane >= c, rolled, 0.0)
            acc[plane + 1, pl.ds(r, extent), :] += jnp.where(lane >= c, 0.0, rolled)

    def measured(slot):
        return jnp.concatenate([patterns_ref[slot, pl.ds(k, extent // 2, stride=2), :] for k in range(2)], axis=0)

    def steps(slots):
        n = range(len(slots))
        field = [[probe[2 * m], probe[2 * m + 1]] for m in modes]
        objects = [window(slot) for slot in slots]
        state = right([[times(field[m], objects[i][0]) for m in modes] for i in n], 1, 0)
        yield
        entering = left(state, 1, 0)
        yield
        state = right([[times(entering[i][m], objects[i][1]) for m in modes] for i in n], 0, 0)
        yield
        state = left(state, 0, 0)
        yield
        weight = [2.0 * (sum(state[i][m][c] * state[i][m][c] for m in modes for c in range(2)) - measured(slots[i]))
                  for i in n]
        state = right([[[weight[i] * state[i][m][c] for c in range(2)] for m in modes] for i in n], 0, 1)
        yield
        state = left(state, 0, 1)
        yield
        for i in n:
            grad = conj_times(entering[i][0], state[i][0])
            for m in modes[1:]:
                grad = add(grad, conj_times(entering[i][m], state[i][m]))
            deposit(slots[i], 1, grad)
        state = right([[conj_times(objects[i][1], state[i][m]) for m in modes] for i in n], 1, 1)
        yield
        state = left(state, 1, 1)
        yield
        for i in n:
            grad = conj_times(field[0], state[i][0])
            for m in modes[1:]:
                grad = add(grad, conj_times(field[m], state[i][m]))
            deposit(slots[i], 0, grad)
        for m in modes:
            term = conj_times(objects[0][0], state[0][m])
            for i in n[1:]:
                term = add(term, conj_times(objects[i][0], state[i][m]))
            probe_acc[2 * m] += term[0]
            probe_acc[2 * m + 1] += term[1]

    def run(*sets):
        running = [steps(slots) for slots in sets]
        while running:
            running = [r for r in running if next(r, "done") is None]

    count = scalars_ref[2 * most]
    fours = lax.shift_right_logical(count, 2)

    def four(j, carry):
        run([4 * j, 4 * j + 1], [4 * j + 2, 4 * j + 3])
        return carry

    lax.fori_loop(0, fours, four, 0)

    @pl.when(lax.bitwise_and(count, 2) == 2)
    def _():
        run([4 * fours], [4 * fours + 1])

    @pl.when(lax.bitwise_and(count, 1) == 1)
    def _():
        run([count - 1])

    for layer in range(SLICES):
        for half in range(HALVES):
            for part in range(2):
                target = (layer * HALVES + half) * 2 + part
                plane = (layer * 2 + part) * HALVES + half
                own_out[pl.ds(target, tile_rows, stride=8), :] = acc[plane, :tile_rows]
                next_out[pl.ds(target, extent, stride=8), :] = acc[plane, tile_rows:]


def prepared(own, patterns):
    extent = patterns.shape[1]
    vmem = pl.BlockSpec(memory_space=pltpu.VMEM)
    parts = jnp.asarray(factors(extent))
    return pl.pallas_call(
        prepare,
        out_shape=(
            jax.ShapeDtypeStruct((8, own.shape[0] // 8, own.shape[1]), jnp.float32),
            jax.ShapeDtypeStruct(patterns.shape, jnp.float32),
            jax.ShapeDtypeStruct((8, 2 * extent, 2 * extent), jnp.bfloat16),
            jax.ShapeDtypeStruct((8, 2 * extent, 2 * extent), jnp.bfloat16),
        ),
        in_specs=[pl.BlockSpec(memory_space=pltpu.HBM)] * 3,
        out_specs=(vmem,) * 4,
        scratch_shapes=[
            pltpu.VMEM(own.shape, jnp.float32),
            pltpu.VMEM(parts.shape, jnp.float32),
            pltpu.SemaphoreType.DMA((3,)),
        ],
        compiler_params=pltpu.CompilerParams(vmem_limit_bytes=16 * 1024 * 1024),
        cost_estimate=pl.CostEstimate(flops=0, bytes_accessed=6 * 1024 * 1024, transcendentals=0),
    )(own, patterns, parts)


def terms(scalars, planes, low, high, near, far, patterns, mats):
    extent = patterns.shape[1]
    rows = planes.shape[1] + extent
    smem = pl.BlockSpec(memory_space=pltpu.SMEM)
    vmem = pl.BlockSpec(memory_space=pltpu.VMEM)
    return pl.pallas_call(
        kernel,
        out_shape=(
            jax.ShapeDtypeStruct((planes.shape[1] * 8, extent), jnp.float32),
            jax.ShapeDtypeStruct((extent * 8, extent), jnp.float32),
            jax.ShapeDtypeStruct((2 * MODES, extent, extent), jnp.float32),
        ),
        in_specs=[smem] + [vmem] * 8,
        out_specs=(vmem,) * 3,
        scratch_shapes=[
            pltpu.VMEM((8, rows, extent), jnp.float32),
            pltpu.VMEM((8, rows, extent), jnp.float32),
            pltpu.VMEM((2 * MODES, extent, extent), jnp.float32),
        ],
        compiler_params=pltpu.CompilerParams(vmem_limit_bytes=40 * 1024 * 1024),
    )(scalars, planes, low, high, near, far, patterns, *mats)


def placed(probe_grad, shape):
    vmem = pl.BlockSpec(memory_space=pltpu.VMEM)
    return pl.pallas_call(
        place,
        out_shape=(jax.ShapeDtypeStruct(shape, jnp.float32),) * 2,
        in_specs=[vmem],
        out_specs=(vmem,) * 2,
        compiler_params=pltpu.CompilerParams(vmem_limit_bytes=4 * 1024 * 1024),
    )(probe_grad)


def flat(block):
    rows, k, parts, columns = block.shape
    split_up = block.reshape(rows, k, parts, columns // 128, 128)
    return split_up.transpose(0, 1, 3, 2, 4).reshape(-1, 128)


def unflat(value, shape):
    rows, k, parts, columns = shape
    return value.reshape(rows, k, columns // 128, parts, 128).transpose(0, 1, 3, 2, 4).reshape(shape)


def partner(value, bits):
    return lax.ppermute(value, "tile", [(i, i ^ bits) for i in range(lax.axis_size("tile"))])


def halved(value):
    return value[:value.shape[0] // 2], value[value.shape[0] // 2:]


def places_on(value, distance):
    members = range(lax.axis_size("tile"))
    return lax.ppermute(value, "tile", [
        (i, i // GROUP_DEV * GROUP_DEV + (i + distance) % GROUP_DEV) for i in members])


def probe_share(probe_grad, shape):
    keep, send = placed(probe_grad, shape)
    blocks = jnp.split(keep + partner(send, 1), 4, axis=0)
    total = blocks[0] + sum(places_on(block, 4 * k) for k, block in enumerate(blocks) if k > 0)
    keep, send = halved(total)
    return keep + partner(send, 2)


def shards(object_slices, probe_field, patterns, row_offsets, col_offsets, counts):
    size = lax.axis_size("tile")
    down = [((i + 1) % size, i) for i in range(size)]
    own = flat(object_slices)
    low, high = halved(own)
    scalars = jnp.concatenate([row_offsets, col_offsets, counts])

    low, high, mine = lax.optimization_barrier((low, high, flat(probe_field)))
    low = lax.ppermute(low, "tile", down)
    quarter = jnp.concatenate([mine, partner(mine, 8), partner(mine, 4), partner(mine, 12)], axis=0)
    low, high, quarter, patterns, own = lax.optimization_barrier((low, high, quarter, patterns, own))
    near = jnp.concatenate([quarter, partner(quarter, 2)], axis=0)
    high = lax.ppermute(high, "tile", down)
    planes, patterns, *mats = prepared(own, patterns)
    near, planes, patterns, scalars, *mats = lax.optimization_barrier((near, planes, patterns, scalars, *mats))
    far = partner(near, 1)

    own_grad, back, probe_grad = terms(scalars, planes, low, high, near, far, patterns, mats)

    back = lax.ppermute(back, "tile", [(i, (i + 1) % size) for i in range(size)])
    probe_sum = lax.cond(
        counts[0] > 0,
        lambda grad: probe_share(grad, near.shape),
        lambda grad: jnp.zeros((near.shape[0] // 8, near.shape[1]), jnp.float32),
        probe_grad)
    object_grad = own_grad + back
    return unflat(object_grad, object_slices.shape), unflat(probe_sum, probe_field.shape)


def solution(mesh):
    in_specs = (
        P(("groups", "tile"), None, None, None),
        P(("groups", "tile"), None, None, None),
        P(("groups", "tile"), None, None),
        P(("groups", "tile")),
        P(("groups", "tile")),
        P(("groups", "tile")),
    )
    out_specs = (P(("groups", "tile"), None, None, None), P(("groups", "tile"), None, None, None))
    return jax.shard_map(shards, mesh=mesh, in_specs=in_specs, out_specs=out_specs, check_vma=False)
```

profile of v0, /device:TPU:0, one launch (start us, length us, event | category | flops | bytes accessed | tf_op | source)
XLA Modules:
  0.0 52.8 jit_solution(7478202290311145187)
XLA Ops:
  0.6 0.0 copy-start.4
  0.6 0.0 copy-start
  0.6 1.2 %fusion.1 = (f32[64,2,2,2,128]{4,3,2,1,0:T(2,128)S(1)}, f32[64,2,2,2,128]{4,3,2,1,0:T(2,128)S(1)}) fusion(f32[128,2,2,2,128]{4,3,2,1,0:T(2,128)} %bitcast.15), kind=kLoop, calls=%fused_computation.6 | loop fusion | bytes 1048576 | tf_op jit(solution)/shard_map/slice | solution.py:327
  1.9 5.5 %collective-permute-start.5 = (f32[512,128]{1,0:T(8,128)S(1)}, f32[512,128]{1,0:T(8,128)S(1)}, u32[]{:S(2)}, u32[]{:S(2)}) collective-permute-start(f32[512,128]{1,0:T(8,128)S(1)} %bitcast.19), channel_id=1, source_target_pairs={{1,0},{2,1},{3,2},{4,3},{5,4},{6,5},{7,6},{8,7},{9,8},{10,9},{11,1... | collective-permute-start | bytes 786440 | tf_op jit(solution)/shard_map/ppermute | solution.py:352
  7.3 0.0 copy-done.4
  7.3 0.4 collective-permute-start.8
  7.8 0.0 collective-permute-start.7
  7.8 3.9 %collective-permute-start.6 = (f32[32,128]{1,0:T(8,128)S(1)}, f32[32,128]{1,0:T(8,128)S(1)}, u32[]{:S(2)}, u32[]{:S(2)}) collective-permute-start(f32[32,128]{1,0:T(8,128)S(1)} %bitcast.23), channel_id=1, source_target_pairs={{0,8},{1,9},{2,10},{3,11},{4,12},{5,13},{6,14},{7,15},{8,0},{9,1},... | collective-permute-start | bytes 49160 | tf_op jit(solution)/shard_map/ppermute | solution.py:323
  12.4 0.5 collective-permute-done.8
  12.9 0.0 collective-permute-done.7
  12.9 0.6 %collective-permute-done.6 = f32[32,128]{1,0:T(8,128)S(1)} collective-permute-done((f32[32,128]{1,0:T(8,128)S(1)}, f32[32,128]{1,0:T(8,128)S(1)}, u32[]{:S(2)}, u32[]{:S(2)}) %collective-permute-start.6) | collective-permute-done | bytes 16416 | tf_op jit(solution)/shard_map/ppermute | solution.py:323
  13.5 0.0 copy-start.5
  13.5 0.0 copy-start.6
  13.5 0.0 collective-permute-done.5.low_ref
  13.5 0.1 collective-permute-start.9
  13.6 2.4 %collective-permute-start.10 = (f32[512,128]{1,0:T(8,128)S(1)}, f32[512,128]{1,0:T(8,128)S(1)}, u32[]{:S(2)}, u32[]{:S(2)}) collective-permute-start(f32[512,128]{1,0:T(8,128)S(1)} %bitcast.18), channel_id=1, source_target_pairs={{1,0},{2,1},{3,2},{4,3},{5,4},{6,5},{7,6},{8,7},{9,8},{10,9},{11,1... | collective-permute-start | bytes 786440 | tf_op jit(solution)/shard_map/ppermute | solution.py:356
  15.9 0.0 copy-done.5
  15.9 0.0 copy-done.6
  15.9 0.1 pad_add_fusion.scalars_ref
  16.0 0.0 copy-done
  16.0 0.0 copy-start.1
  16.0 1.2 %copy-done.1 = f32[16,128,128]{2,1,0:T(8,128)S(1)} copy-done((f32[16,128,128]{2,1,0:T(8,128)S(1)}, f32[16,128,128]{2,1,0:T(8,128)}, u32[]{:S(2)}) %copy-start.1) | copy-done | bytes 1048600
  17.2 0.0 copy-start.2
  17.2 1.1 %copy-done.2 = f32[12,128,128]{2,1,0:T(8,128)S(1)} copy-done((f32[12,128,128]{2,1,0:T(8,128)S(1)}, f32[12,128,128]{2,1,0:T(8,128)}, u32[]{:S(2)}) %copy-start.2) | copy-done | bytes 786456
  18.4 0.6 %shard_map.86 = (f32[8,128,128]{2,1,0:T(8,128)S(1)}, f32[16,128,128]{2,1,0:T(8,128)S(1)}, bf16[8,256,256]{2,1,0:T(8,128)(2,1)S(1)}, bf16[8,256,256]{2,1,0:T(8,128)(2,1)S(1)}) custom-call(f32[1024,128]{1,0:T(8,128)S(1)} %bitcast.16, f32[16,128,128]{2,1,0:T(8,128)S(1)} %copy-done.1, f32[12,128,128]{2,1,0:T(8,128)S(1)} %copy-done.2), custom_call_target="tpu_custom_call" | custom-call | bytes 6291456 | tf_op jit(solution)/shard_map/pallas_call | solution.py:257
  18.9 0.0 collective-permute-done.9
  19.0 0.1 collective-permute-start.11
  19.0 1.3 %collective-permute-done.11.far_ref = f32[256,128]{1,0:T(8,128)S(1)} collective-permute-done((f32[256,128]{1,0:T(8,128)S(1)}, f32[256,128]{1,0:T(8,128)S(1)}, u32[]{:S(2)}, u32[]{:S(2)}) %collective-permute-start.11) | collective-permute-done | bytes 131104 | tf_op jit(solution)/shard_map/ppermute | solution.py:323
  20.4 0.0 collective-permute-done.10.high_ref
  20.4 7.7 %shard_map.87 = (f32[1024,128]{1,0:T(8,128)S(1)}, f32[1024,128]{1,0:T(8,128)S(1)}, f32[4,128,128]{2,1,0:T(8,128)S(1)}) custom-call(s32[33]{0:T(128)S(1)} %pad_add_fusion.scalars_ref, f32[8,128,128]{2,1,0:T(8,128)S(1)} %get-tuple-element.41.own_ref, f32[512,128]{1,0:T(8,128)S(1)} %collective-permute-done.5.low_ref, ...), custom_call_target="tpu_custom_call" | custom-call | tf_op jit(solution)/shard_map/pallas_call | solution.py:282
  28.1 0.3 collective-permute-start.12
  28.4 23.5 %conditional.1 = (f32[8,2,2,128]{3,2,1,0:T(2,128)S(1)}) conditional(s32[]{:T(128)} %bitcast.11, () %tuple.22, f32[4,128,128]{2,1,0:T(8,128)S(1)} %get-tuple-element.50), branch_computations={%region_0.0_spmd, %region_1.0_spmd} | conditional | flops 61440 | bytes 1818832 | solution.py:364
  28.5 0.1 collective-permute-start
  28.6 1.6 %collective-permute-done = f32[256,128]{1,0:T(8,128)S(1)} collective-permute-done((f32[256,128]{1,0:T(8,128)S(1)}, f32[256,128]{1,0:T(8,128)S(1)}, u32[]{:S(2)}, u32[]{:S(2)}) %collective-permute-start) | collective-permute-done | bytes 131104 | tf_op jit(solution)/shard_map/cond/branch_1_fun/ppermute | solution.py:323
  30.2 1.0 %collective-permute-start.2 = (f32[64,128]{1,0:T(8,128)S(1)}, f32[64,128]{1,0:T(8,128)S(1)}, u32[]{:S(2)}, u32[]{:S(2)}) collective-permute-start(f32[64,128]{1,0:T(8,128)S(1)} %get-tuple-element.51), channel_id=1, source_target_pairs={{0,8},{1,9},{2,10},{3,11},{4,12},{5,13},{6,14},{7,15},{8,0},{9,1},... | collective-permute-start | bytes 98312 | tf_op jit(solution)/shard_map/cond/branch_1_fun/ppermute | solution.py:332
  31.2 11.1 %collective-permute-start.3 = (f32[64,128]{1,0:T(8,128)S(1)}, f32[64,128]{1,0:T(8,128)S(1)}, u32[]{:S(2)}, u32[]{:S(2)}) collective-permute-start(f32[64,128]{1,0:T(8,128)S(1)} %get-tuple-element.52), channel_id=1, source_target_pairs={{0,12},{1,13},{2,14},{3,15},{4,0},{5,1},{6,2},{7,3},{8,4},{9,5},{1... | collective-permute-start | bytes 98312 | tf_op jit(solution)/shard_map/cond/branch_1_fun/ppermute | solution.py:332
  42.4 0.0 collective-permute-start.1
  42.4 0.0 collective-permute-done.2
  42.4 1.6 %collective-permute-done.3 = f32[64,128]{1,0:T(8,128)S(1)} collective-permute-done((f32[64,128]{1,0:T(8,128)S(1)}, f32[64,128]{1,0:T(8,128)S(1)}, u32[]{:S(2)}, u32[]{:S(2)}) %collective-permute-start.3) | collective-permute-done | bytes 32800 | tf_op jit(solution)/shard_map/cond/branch_1_fun/ppermute | solution.py:332
  44.0 4.1 %collective-permute-done.1 = f32[64,128]{1,0:T(8,128)S(1)} collective-permute-done((f32[64,128]{1,0:T(8,128)S(1)}, f32[64,128]{1,0:T(8,128)S(1)}, u32[]{:S(2)}, u32[]{:S(2)}) %collective-permute-start.1) | collective-permute-done | bytes 32800 | tf_op jit(solution)/shard_map/cond/branch_1_fun/ppermute | solution.py:332
  48.1 0.6 %collective-permute-start.4 = (f32[32,128]{1,0:T(8,128)S(1)}, f32[32,128]{1,0:T(8,128)S(1)}, u32[]{:S(2)}, u32[]{:S(2)}) collective-permute-start(f32[32,128]{1,0:T(8,128)S(1)} %slice.23), channel_id=1, source_target_pairs={{0,2},{1,3},{2,0},{3,1},{4,6},{5,7},{6,4},{7,5},{8,10},{9,11},{10,... | collective-permute-start | bytes 49160 | tf_op jit(solution)/shard_map/cond/branch_1_fun/ppermute | solution.py:323
  48.7 3.2 %collective-permute-done.4 = f32[32,128]{1,0:T(8,128)S(1)} collective-permute-done((f32[32,128]{1,0:T(8,128)S(1)}, f32[32,128]{1,0:T(8,128)S(1)}, u32[]{:S(2)}, u32[]{:S(2)}) %collective-permute-start.4) | collective-permute-done | bytes 16416 | tf_op jit(solution)/shard_map/cond/branch_1_fun/ppermute | solution.py:323
  51.9 0.0 copy-start.3
  51.9 0.0 collective-permute-done.12
  51.9 0.8 %add.18 = f32[1024,128]{1,0:T(8,128)} add(f32[1024,128]{1,0:T(8,128)S(1)} %get-tuple-element.48, f32[1024,128]{1,0:T(8,128)S(1)} %collective-permute-done.12) | non-fusion elementwise | flops 131072 | bytes 1572864 | tf_op jit(solution)/shard_map/add | solution.py:369
  52.8 0.0 copy-done.3
  (8 shorter events, 0.1 us)
Async XLA Ops:
  0.6 6.7 %copy-start.4 = (f32[8,2,2,128]{3,2,1,0:T(2,128)S(1)}, f32[8,2,2,128]{3,2,1,0:T(2,128)}, u32[]{:S(2)}) copy-start(f32[8,2,2,128]{3,2,1,0:T(2,128)} %param.10) | copy-start | bytes 49156
  0.6 15.4 %copy-start = (f32[128,2,2,256]{3,2,1,0:T(2,128)S(1)}, f32[128,2,2,256]{3,2,1,0:T(2,128)}, u32[]{:S(2)}) copy-start(f32[128,2,2,256]{3,2,1,0:T(2,128)} %param.9) | copy-start | bytes 1572868
  1.9 11.6 %collective-permute-start.5 = (f32[512,128]{1,0:T(8,128)S(1)}, f32[512,128]{1,0:T(8,128)S(1)}, u32[]{:S(2)}, u32[]{:S(2)}) collective-permute-start(f32[512,128]{1,0:T(8,128)S(1)} %bitcast.19), channel_id=1, source_target_pairs={{1,0},{2,1},{3,2},{4,3},{5,4},{6,5},{7,6},{8,7},{9,8},{10,9},{11,1... | collective-permute-start | bytes 786440 | tf_op jit(solution)/shard_map/ppermute | solution.py:352
  7.3 5.5 %collective-permute-start.8 = (f32[32,128]{1,0:T(8,128)S(1)}, f32[32,128]{1,0:T(8,128)S(1)}, u32[]{:S(2)}, u32[]{:S(2)}) collective-permute-start(f32[32,128]{1,0:T(8,128)S(1)} %bitcast.21), channel_id=1, source_target_pairs={{0,12},{1,13},{2,14},{3,15},{4,8},{5,9},{6,10},{7,11},{8,4},{9,5},... | collective-permute-start | bytes 49160 | tf_op jit(solution)/shard_map/ppermute | solution.py:323
  7.8 5.1 %collective-permute-start.7 = (f32[32,128]{1,0:T(8,128)S(1)}, f32[32,128]{1,0:T(8,128)S(1)}, u32[]{:S(2)}, u32[]{:S(2)}) collective-permute-start(f32[32,128]{1,0:T(8,128)S(1)} %bitcast.22), channel_id=1, source_target_pairs={{0,4},{1,5},{2,6},{3,7},{4,0},{5,1},{6,2},{7,3},{8,12},{9,13},{10,... | collective-permute-start | bytes 49160 | tf_op jit(solution)/shard_map/ppermute | solution.py:323
  7.8 5.7 %collective-permute-start.6 = (f32[32,128]{1,0:T(8,128)S(1)}, f32[32,128]{1,0:T(8,128)S(1)}, u32[]{:S(2)}, u32[]{:S(2)}) collective-permute-start(f32[32,128]{1,0:T(8,128)S(1)} %bitcast.23), channel_id=1, source_target_pairs={{0,8},{1,9},{2,10},{3,11},{4,12},{5,13},{6,14},{7,15},{8,0},{9,1},... | collective-permute-start | bytes 49160 | tf_op jit(solution)/shard_map/ppermute | solution.py:323
  13.5 2.5 %copy-start.5 = (s32[16]{0:T(128)S(1)}, s32[16]{0:T(128)}, u32[]{:S(2)}) copy-start(s32[16]{0:T(128)} %param.13) | copy-start | bytes 196
  13.5 2.5 %copy-start.6 = (s32[16]{0:T(128)S(1)}, s32[16]{0:T(128)}, u32[]{:S(2)}) copy-start(s32[16]{0:T(128)} %param.12) | copy-start | bytes 196
  13.5 5.5 %collective-permute-start.9 = (f32[128,128]{1,0:T(8,128)S(1)}, f32[128,128]{1,0:T(8,128)S(1)}, u32[]{:S(2)}, u32[]{:S(2)}) collective-permute-start(f32[128,128]{1,0:T(8,128)S(1)} %pad_maximum_fusion.1), channel_id=1, source_target_pairs={{0,2},{1,3},{2,0},{3,1},{4,6},{5,7},{6,4},{7,5},{8,10},{9,11},{10,... | collective-permute-start | bytes 196616 | tf_op jit(solution)/shard_map/ppermute | solution.py:323
  13.6 6.8 %collective-permute-start.10 = (f32[512,128]{1,0:T(8,128)S(1)}, f32[512,128]{1,0:T(8,128)S(1)}, u32[]{:S(2)}, u32[]{:S(2)}) collective-permute-start(f32[512,128]{1,0:T(8,128)S(1)} %bitcast.18), channel_id=1, source_target_pairs={{1,0},{2,1},{3,2},{4,3},{5,4},{6,5},{7,6},{8,7},{9,8},{10,9},{11,1... | collective-permute-start | bytes 786440 | tf_op jit(solution)/shard_map/ppermute | solution.py:356
  16.0 1.2 %copy-start.1 = (f32[16,128,128]{2,1,0:T(8,128)S(1)}, f32[16,128,128]{2,1,0:T(8,128)}, u32[]{:S(2)}) copy-start(f32[16,128,128]{2,1,0:T(8,128)} %patterns_ref) | copy-start | bytes 3145732
  17.2 1.1 %copy-start.2 = (f32[12,128,128]{2,1,0:T(8,128)S(1)}, f32[12,128,128]{2,1,0:T(8,128)}, u32[]{:S(2)}) copy-start(f32[12,128,128]{2,1,0:T(8,128)} %constant.7.clone.factors_ref) | copy-start | bytes 2359300
  19.0 1.4 %collective-permute-start.11 = (f32[256,128]{1,0:T(8,128)S(1)}, f32[256,128]{1,0:T(8,128)S(1)}, u32[]{:S(2)}, u32[]{:S(2)}) collective-permute-start(f32[256,128]{1,0:T(8,128)S(1)} %pad_maximum_fusion.near_ref), channel_id=1, source_target_pairs={{0,1},{1,0},{2,3},{3,2},{4,5},{5,4},{6,7},{7,6},{8,9},{9,8},{10,11... | collective-permute-start | bytes 393224 | tf_op jit(solution)/shard_map/ppermute | solution.py:323
  28.1 23.8 %collective-permute-start.12 = (f32[1024,128]{1,0:T(8,128)S(1)}, f32[1024,128]{1,0:T(8,128)S(1)}, u32[]{:S(2)}, u32[]{:S(2)}) collective-permute-start(f32[1024,128]{1,0:T(8,128)S(1)} %get-tuple-element.49), channel_id=1, source_target_pairs={{0,1},{1,2},{2,3},{3,4},{4,5},{5,6},{6,7},{7,8},{8,9},{9,10},{10,1... | collective-permute-start | bytes 1572872 | tf_op jit(solution)/shard_map/ppermute | solution.py:363
  28.5 1.7 %collective-permute-start = (f32[256,128]{1,0:T(8,128)S(1)}, f32[256,128]{1,0:T(8,128)S(1)}, u32[]{:S(2)}, u32[]{:S(2)}) collective-permute-start(f32[256,128]{1,0:T(8,128)S(1)} %get-tuple-element.6), channel_id=1, source_target_pairs={{0,1},{1,0},{2,3},{3,2},{4,5},{5,4},{6,7},{7,6},{8,9},{9,8},{10,11... | collective-permute-start | bytes 393224 | tf_op jit(solution)/shard_map/cond/branch_1_fun/ppermute | solution.py:323
  30.2 12.2 %collective-permute-start.2 = (f32[64,128]{1,0:T(8,128)S(1)}, f32[64,128]{1,0:T(8,128)S(1)}, u32[]{:S(2)}, u32[]{:S(2)}) collective-permute-start(f32[64,128]{1,0:T(8,128)S(1)} %get-tuple-element.51), channel_id=1, source_target_pairs={{0,8},{1,9},{2,10},{3,11},{4,12},{5,13},{6,14},{7,15},{8,0},{9,1},... | collective-permute-start | bytes 98312 | tf_op jit(solution)/shard_map/cond/branch_1_fun/ppermute | solution.py:332
  31.2 12.7 %collective-permute-start.3 = (f32[64,128]{1,0:T(8,128)S(1)}, f32[64,128]{1,0:T(8,128)S(1)}, u32[]{:S(2)}, u32[]{:S(2)}) collective-permute-start(f32[64,128]{1,0:T(8,128)S(1)} %get-tuple-element.52), channel_id=1, source_target_pairs={{0,12},{1,13},{2,14},{3,15},{4,0},{5,1},{6,2},{7,3},{8,4},{9,5},{1... | collective-permute-start | bytes 98312 | tf_op jit(solution)/shard_map/cond/branch_1_fun/ppermute | solution.py:332
  42.4 5.7 %collective-permute-start.1 = (f32[64,128]{1,0:T(8,128)S(1)}, f32[64,128]{1,0:T(8,128)S(1)}, u32[]{:S(2)}, u32[]{:S(2)}) collective-permute-start(f32[64,128]{1,0:T(8,128)S(1)} %get-tuple-element.53), channel_id=1, source_target_pairs={{0,4},{1,5},{2,6},{3,7},{4,8},{5,9},{6,10},{7,11},{8,12},{9,13},{1... | collective-permute-start | bytes 98312 | tf_op jit(solution)/shard_map/cond/branch_1_fun/ppermute | solution.py:332
  48.1 3.8 %collective-permute-start.4 = (f32[32,128]{1,0:T(8,128)S(1)}, f32[32,128]{1,0:T(8,128)S(1)}, u32[]{:S(2)}, u32[]{:S(2)}) collective-permute-start(f32[32,128]{1,0:T(8,128)S(1)} %slice.23), channel_id=1, source_target_pairs={{0,2},{1,3},{2,0},{3,1},{4,6},{5,7},{6,4},{7,5},{8,10},{9,11},{10,... | collective-permute-start | bytes 49160 | tf_op jit(solution)/shard_map/cond/branch_1_fun/ppermute | solution.py:323
  51.9 0.9 %copy-start.3 = (f32[8,2,2,128]{3,2,1,0:T(2,128)}, f32[8,2,2,128]{3,2,1,0:T(2,128)S(1)}, u32[]{:S(2)}) copy-start(f32[8,2,2,128]{3,2,1,0:T(2,128)S(1)} %get-tuple-element.56) | copy-start | bytes 49156
where the time goes:
time: 53.6 us; the launch traced here: 52.8 us
  starting transfers between devices  25.6 us (48%)
  waiting for transfers between devices  12.9 us (24%)
  Pallas kernels  8.31 us (16%)
  local copies, waits for them, and re-layouts  3.62 us (7%)
  between operations  1.38 us (3%)
  other arithmetic  0.97 us (2%)
    ppermute x3, starting transfers between devices, places_on(): lax.ppermute(value, 'tile', [(i, i // GROUP_DEV * GROUP_DEV + (i + distan...  12.2 us
    pallas_call x1, Pallas kernels, terms(): pl.pallas_call(kernel, out_shape=(jax.ShapeDtypeStruct((planes.shape[1] *...  7.72 us
    ppermute x7, waiting for transfers between devices, partner(): lax.ppermute(value, 'tile', [(i, i ^ bits) for i in range(lax.axis_size('...  7.18 us
    ppermute x3, waiting for transfers between devices, places_on(): lax.ppermute(value, 'tile', [(i, i // GROUP_DEV * GROUP_DEV + (i + distan...  5.71 us
    ppermute x1, starting transfers between devices, shards(): low = lax.ppermute(low, 'tile', down)  5.47 us
    ppermute x7, starting transfers between devices, partner(): lax.ppermute(value, 'tile', [(i, i ^ bits) for i in range(lax.axis_size('...  5.24 us
    unnamed x14, local copies, waits for them, and re-layouts  2.38 us
    ppermute x1, starting transfers between devices, shards(): high = lax.ppermute(high, 'tile', down)  2.36 us
  transfers between devices with their start and end apart: 13, of which 7 were waited for; matrix products, arithmetic and copies ran while one was open for 0% of the time, Pallas kernels for 1%

commit v1 on v0

--- a/solution.py
+++ b/solution.py
@@ -225,13 +225,19 @@
             running = [r for r in running if next(r, "done") is None]
 
     count = scalars_ref[2 * most]
+    eights = lax.shift_right_logical(count, 3)
     fours = lax.shift_right_logical(count, 2)
+
+    def eight(j, carry):
+        run(*([8 * j + k, 8 * j + k + 1] for k in range(0, 8, 2)))
+        return carry
 
     def four(j, carry):
         run([4 * j, 4 * j + 1], [4 * j + 2, 4 * j + 3])
         return carry
 
-    lax.fori_loop(0, fours, four, 0)
+    lax.fori_loop(0, eights, eight, 0)
+    lax.fori_loop(2 * eights, fours, four, 0)
 
     @pl.when(lax.bitwise_and(count, 2) == 2)
     def _():

time: 53.6 us -> 52.4 us (0.978); the launches traced: 52.8 us -> 53.3 us
  waiting for transfers between devices: 12.9 us -> 10.9 us
  Pallas kernels: 8.31 us -> 9.57 us
  starting transfers between devices: 25.6 us -> 26.8 us
    ppermute x3, waiting for transfers between devices: 5.71 us -> 3.69 us  [places_on(): lax.ppermute(value, 'tile', [(i, i // GROUP_DEV * GROUP_DEV + (i + distan...]
    ppermute x3, starting transfers between devices: 12.2 us -> 13.7 us  [places_on(): lax.ppermute(value, 'tile', [(i, i // GROUP_DEV * GROUP_DEV + (i + distan...]
    pallas_call x1, Pallas kernels: 7.72 us -> 8.96 us  [terms(): pl.pallas_call(kernel, out_shape=(jax.ShapeDtypeStruct((planes.shape[1] *...]
  transfers between devices with their start and end apart: 13 -> 13, of which waited for: 7 -> 8; matrix products, arithmetic and copies ran while one was open for 0% -> 0% of each run, Pallas kernels for 1% -> 1%
where the time goes in v1:
time: 52.4 us; the launch traced here: 53.3 us
  starting transfers between devices  26.8 us (51%)
  waiting for transfers between devices  10.9 us (21%)
  Pallas kernels  9.57 us (18%)
  local copies, waits for them, and re-layouts  3.62 us (7%)
  between operations  1.4 us (3%)
  other arithmetic  0.97 us (2%)
    ppermute x3, starting transfers between devices, places_on(): lax.ppermute(value, 'tile', [(i, i // GROUP_DEV * GROUP_DEV + (i + distan...  13.7 us
    pallas_call x1, Pallas kernels, terms(): pl.pallas_call(kernel, out_shape=(jax.ShapeDtypeStruct((planes.shape[1] *...  8.96 us
    ppermute x7, waiting for transfers between devices, partner(): lax.ppermute(value, 'tile', [(i, i ^ bits) for i in range(lax.axis_size('...  7.17 us
    ppermute x1, starting transfers between devices, shards(): low = lax.ppermute(low, 'tile', down)  5.47 us
    ppermute x7, starting transfers between devices, partner(): lax.ppermute(value, 'tile', [(i, i ^ bits) for i in range(lax.axis_size('...  5.19 us
    ppermute x3, waiting for transfers between devices, places_on(): lax.ppermute(value, 'tile', [(i, i // GROUP_DEV * GROUP_DEV + (i + distan...  3.69 us
    unnamed x14, local copies, waits for them, and re-layouts  2.38 us
    ppermute x1, starting transfers between devices, shards(): high = lax.ppermute(high, 'tile', down)  2.36 us
  transfers between devices with their start and end apart: 13, of which 8 were waited for; matrix products, arithmetic and copies ran while one was open for 0% of the time, Pallas kernels for 1%

profile of v1, /device:TPU:0, one launch (start us, length us, event | category | flops | bytes accessed | tf_op | source)
XLA Modules:
  0.0 53.3 jit_solution(13740090948360613778)
XLA Ops:
  0.6 0.0 copy-start.4
  0.6 0.0 copy-start
  0.6 1.2 %fusion.1 = (f32[64,2,2,2,128]{4,3,2,1,0:T(2,128)S(1)}, f32[64,2,2,2,128]{4,3,2,1,0:T(2,128)S(1)}) fusion(f32[128,2,2,2,128]{4,3,2,1,0:T(2,128)} %bitcast.15), kind=kLoop, calls=%fused_computation.6 | loop fusion | bytes 1048576 | tf_op jit(solution)/shard_map/slice | solution.py:333
  1.9 5.5 %collective-permute-start.5 = (f32[512,128]{1,0:T(8,128)S(1)}, f32[512,128]{1,0:T(8,128)S(1)}, u32[]{:S(2)}, u32[]{:S(2)}) collective-permute-start(f32[512,128]{1,0:T(8,128)S(1)} %bitcast.19), channel_id=1, source_target_pairs={{1,0},{2,1},{3,2},{4,3},{5,4},{6,5},{7,6},{8,7},{9,8},{10,9},{11,1... | collective-permute-start | bytes 786440 | tf_op jit(solution)/shard_map/ppermute | solution.py:358
  7.3 0.0 copy-done.4
  7.3 0.4 collective-permute-start.8
  7.8 0.0 collective-permute-start.7
  7.8 3.9 %collective-permute-start.6 = (f32[32,128]{1,0:T(8,128)S(1)}, f32[32,128]{1,0:T(8,128)S(1)}, u32[]{:S(2)}, u32[]{:S(2)}) collective-permute-start(f32[32,128]{1,0:T(8,128)S(1)} %bitcast.23), channel_id=1, source_target_pairs={{0,8},{1,9},{2,10},{3,11},{4,12},{5,13},{6,14},{7,15},{8,0},{9,1},... | collective-permute-start | bytes 49160 | tf_op jit(solution)/shard_map/ppermute | solution.py:329
  12.4 0.5 collective-permute-done.8
  12.9 0.0 collective-permute-done.7
  12.9 0.6 %collective-permute-done.6 = f32[32,128]{1,0:T(8,128)S(1)} collective-permute-done((f32[32,128]{1,0:T(8,128)S(1)}, f32[32,128]{1,0:T(8,128)S(1)}, u32[]{:S(2)}, u32[]{:S(2)}) %collective-permute-start.6) | collective-permute-done | bytes 16416 | tf_op jit(solution)/shard_map/ppermute | solution.py:329
  13.5 0.0 copy-start.5
  13.5 0.0 copy-start.6
  13.5 0.0 collective-permute-done.5.low_ref
  13.5 0.1 collective-permute-start.9
  13.6 2.4 %collective-permute-start.10 = (f32[512,128]{1,0:T(8,128)S(1)}, f32[512,128]{1,0:T(8,128)S(1)}, u32[]{:S(2)}, u32[]{:S(2)}) collective-permute-start(f32[512,128]{1,0:T(8,128)S(1)} %bitcast.18), channel_id=1, source_target_pairs={{1,0},{2,1},{3,2},{4,3},{5,4},{6,5},{7,6},{8,7},{9,8},{10,9},{11,1... | collective-permute-start | bytes 786440 | tf_op jit(solution)/shard_map/ppermute | solution.py:362
  15.9 0.0 copy-done.5
  15.9 0.0 copy-done.6
  15.9 0.1 pad_add_fusion.scalars_ref
  16.0 0.0 copy-done
  16.0 0.0 copy-start.1
  16.0 1.2 %copy-done.1 = f32[16,128,128]{2,1,0:T(8,128)S(1)} copy-done((f32[16,128,128]{2,1,0:T(8,128)S(1)}, f32[16,128,128]{2,1,0:T(8,128)}, u32[]{:S(2)}) %copy-start.1) | copy-done | bytes 1048600
  17.2 0.0 copy-start.2
  17.2 1.1 %copy-done.2 = f32[12,128,128]{2,1,0:T(8,128)S(1)} copy-done((f32[12,128,128]{2,1,0:T(8,128)S(1)}, f32[12,128,128]{2,1,0:T(8,128)}, u32[]{:S(2)}) %copy-start.2) | copy-done | bytes 786456
  18.4 0.6 %shard_map.86 = (f32[8,128,128]{2,1,0:T(8,128)S(1)}, f32[16,128,128]{2,1,0:T(8,128)S(1)}, bf16[8,256,256]{2,1,0:T(8,128)(2,1)S(1)}, bf16[8,256,256]{2,1,0:T(8,128)(2,1)S(1)}) custom-call(f32[1024,128]{1,0:T(8,128)S(1)} %bitcast.16, f32[16,128,128]{2,1,0:T(8,128)S(1)} %copy-done.1, f32[12,128,128]{2,1,0:T(8,128)S(1)} %copy-done.2), custom_call_target="tpu_custom_call" | custom-call | bytes 6291456 | tf_op jit(solution)/shard_map/pallas_call | solution.py:263
  18.9 0.0 collective-permute-done.9
  19.0 0.1 collective-permute-start.11
  19.0 1.3 %collective-permute-done.11.far_ref = f32[256,128]{1,0:T(8,128)S(1)} collective-permute-done((f32[256,128]{1,0:T(8,128)S(1)}, f32[256,128]{1,0:T(8,128)S(1)}, u32[]{:S(2)}, u32[]{:S(2)}) %collective-permute-start.11) | collective-permute-done | bytes 131104 | tf_op jit(solution)/shard_map/ppermute | solution.py:329
  20.4 0.0 collective-permute-done.10.high_ref
  20.4 9.0 %shard_map.87 = (f32[1024,128]{1,0:T(8,128)S(1)}, f32[1024,128]{1,0:T(8,128)S(1)}, f32[4,128,128]{2,1,0:T(8,128)S(1)}) custom-call(s32[33]{0:T(128)S(1)} %pad_add_fusion.scalars_ref, f32[8,128,128]{2,1,0:T(8,128)S(1)} %get-tuple-element.41.own_ref, f32[512,128]{1,0:T(8,128)S(1)} %collective-permute-done.5.low_ref, ...), custom_call_target="tpu_custom_call" | custom-call | tf_op jit(solution)/shard_map/pallas_call | solution.py:288
  29.4 0.1 collective-permute-start.12
  29.4 23.0 %conditional.1 = (f32[8,2,2,128]{3,2,1,0:T(2,128)S(1)}) conditional(s32[]{:T(128)} %bitcast.11, () %tuple.22, f32[4,128,128]{2,1,0:T(8,128)S(1)} %get-tuple-element.50), branch_computations={%region_0.0_spmd, %region_1.0_spmd} | conditional | flops 61440 | bytes 1818832 | solution.py:370
  29.5 0.1 collective-permute-start
  29.6 1.6 %collective-permute-done = f32[256,128]{1,0:T(8,128)S(1)} collective-permute-done((f32[256,128]{1,0:T(8,128)S(1)}, f32[256,128]{1,0:T(8,128)S(1)}, u32[]{:S(2)}, u32[]{:S(2)}) %collective-permute-start) | collective-permute-done | bytes 131104 | tf_op jit(solution)/shard_map/cond/branch_1_fun/ppermute | solution.py:329
  31.2 11.7 %collective-permute-start.2 = (f32[64,128]{1,0:T(8,128)S(1)}, f32[64,128]{1,0:T(8,128)S(1)}, u32[]{:S(2)}, u32[]{:S(2)}) collective-permute-start(f32[64,128]{1,0:T(8,128)S(1)} %get-tuple-element.51), channel_id=1, source_target_pairs={{0,8},{1,9},{2,10},{3,11},{4,12},{5,13},{6,14},{7,15},{8,0},{9,1},... | collective-permute-start | bytes 98312 | tf_op jit(solution)/shard_map/cond/branch_1_fun/ppermute | solution.py:338
  42.9 0.0 collective-permute-start.3
  42.9 2.0 %collective-permute-start.1 = (f32[64,128]{1,0:T(8,128)S(1)}, f32[64,128]{1,0:T(8,128)S(1)}, u32[]{:S(2)}, u32[]{:S(2)}) collective-permute-start(f32[64,128]{1,0:T(8,128)S(1)} %get-tuple-element.53), channel_id=1, source_target_pairs={{0,4},{1,5},{2,6},{3,7},{4,8},{5,9},{6,10},{7,11},{8,12},{9,13},{1... | collective-permute-start | bytes 98312 | tf_op jit(solution)/shard_map/cond/branch_1_fun/ppermute | solution.py:338
  44.9 0.2 collective-permute-done.2
  45.1 1.7 %collective-permute-done.3 = f32[64,128]{1,0:T(8,128)S(1)} collective-permute-done((f32[64,128]{1,0:T(8,128)S(1)}, f32[64,128]{1,0:T(8,128)S(1)}, u32[]{:S(2)}, u32[]{:S(2)}) %collective-permute-start.3) | collective-permute-done | bytes 32800 | tf_op jit(solution)/shard_map/cond/branch_1_fun/ppermute | solution.py:338
  46.8 1.8 %collective-permute-done.1 = f32[64,128]{1,0:T(8,128)S(1)} collective-permute-done((f32[64,128]{1,0:T(8,128)S(1)}, f32[64,128]{1,0:T(8,128)S(1)}, u32[]{:S(2)}, u32[]{:S(2)}) %collective-permute-start.1) | collective-permute-done | bytes 32800 | tf_op jit(solution)/shard_map/cond/branch_1_fun/ppermute | solution.py:338
  48.6 0.6 %collective-permute-start.4 = (f32[32,128]{1,0:T(8,128)S(1)}, f32[32,128]{1,0:T(8,128)S(1)}, u32[]{:S(2)}, u32[]{:S(2)}) collective-permute-start(f32[32,128]{1,0:T(8,128)S(1)} %slice.23), channel_id=1, source_target_pairs={{0,2},{1,3},{2,0},{3,1},{4,6},{5,7},{6,4},{7,5},{8,10},{9,11},{10,... | collective-permute-start | bytes 49160 | tf_op jit(solution)/shard_map/cond/branch_1_fun/ppermute | solution.py:329
  49.2 3.2 %collective-permute-done.4 = f32[32,128]{1,0:T(8,128)S(1)} collective-permute-done((f32[32,128]{1,0:T(8,128)S(1)}, f32[32,128]{1,0:T(8,128)S(1)}, u32[]{:S(2)}, u32[]{:S(2)}) %collective-permute-start.4) | collective-permute-done | bytes 16416 | tf_op jit(solution)/shard_map/cond/branch_1_fun/ppermute | solution.py:329
  52.4 0.0 copy-start.3
  52.4 0.0 collective-permute-done.12
  52.4 0.8 %add.18 = f32[1024,128]{1,0:T(8,128)} add(f32[1024,128]{1,0:T(8,128)S(1)} %get-tuple-element.48, f32[1024,128]{1,0:T(8,128)S(1)} %collective-permute-done.12) | non-fusion elementwise | flops 131072 | bytes 1572864 | tf_op jit(solution)/shard_map/add | solution.py:375
  53.3 0.0 copy-done.3
  (8 shorter events, 0.1 us)
Async XLA Ops:
  0.6 6.7 %copy-start.4 = (f32[8,2,2,128]{3,2,1,0:T(2,128)S(1)}, f32[8,2,2,128]{3,2,1,0:T(2,128)}, u32[]{:S(2)}) copy-start(f32[8,2,2,128]{3,2,1,0:T(2,128)} %param.10) | copy-start | bytes 49156
  0.6 15.4 %copy-start = (f32[128,2,2,256]{3,2,1,0:T(2,128)S(1)}, f32[128,2,2,256]{3,2,1,0:T(2,128)}, u32[]{:S(2)}) copy-start(f32[128,2,2,256]{3,2,1,0:T(2,128)} %param.9) | copy-start | bytes 1572868
  1.9 11.6 %collective-permute-start.5 = (f32[512,128]{1,0:T(8,128)S(1)}, f32[512,128]{1,0:T(8,128)S(1)}, u32[]{:S(2)}, u32[]{:S(2)}) collective-permute-start(f32[512,128]{1,0:T(8,128)S(1)} %bitcast.19), channel_id=1, source_target_pairs={{1,0},{2,1},{3,2},{4,3},{5,4},{6,5},{7,6},{8,7},{9,8},{10,9},{11,1... | collective-permute-start | bytes 786440 | tf_op jit(solution)/shard_map/ppermute | solution.py:358
  7.3 5.5 %collective-permute-start.8 = (f32[32,128]{1,0:T(8,128)S(1)}, f32[32,128]{1,0:T(8,128)S(1)}, u32[]{:S(2)}, u32[]{:S(2)}) collective-permute-start(f32[32,128]{1,0:T(8,128)S(1)} %bitcast.21), channel_id=1, source_target_pairs={{0,12},{1,13},{2,14},{3,15},{4,8},{5,9},{6,10},{7,11},{8,4},{9,5},... | collective-permute-start | bytes 49160 | tf_op jit(solution)/shard_map/ppermute | solution.py:329
  7.8 5.1 %collective-permute-start.7 = (f32[32,128]{1,0:T(8,128)S(1)}, f32[32,128]{1,0:T(8,128)S(1)}, u32[]{:S(2)}, u32[]{:S(2)}) collective-permute-start(f32[32,128]{1,0:T(8,128)S(1)} %bitcast.22), channel_id=1, source_target_pairs={{0,4},{1,5},{2,6},{3,7},{4,0},{5,1},{6,2},{7,3},{8,12},{9,13},{10,... | collective-permute-start | bytes 49160 | tf_op jit(solution)/shard_map/ppermute | solution.py:329
  7.8 5.7 %collective-permute-start.6 = (f32[32,128]{1,0:T(8,128)S(1)}, f32[32,128]{1,0:T(8,128)S(1)}, u32[]{:S(2)}, u32[]{:S(2)}) collective-permute-start(f32[32,128]{1,0:T(8,128)S(1)} %bitcast.23), channel_id=1, source_target_pairs={{0,8},{1,9},{2,10},{3,11},{4,12},{5,13},{6,14},{7,15},{8,0},{9,1},... | collective-permute-start | bytes 49160 | tf_op jit(solution)/shard_map/ppermute | solution.py:329
  13.5 2.5 %copy-start.5 = (s32[16]{0:T(128)S(1)}, s32[16]{0:T(128)}, u32[]{:S(2)}) copy-start(s32[16]{0:T(128)} %param.13) | copy-start | bytes 196
  13.5 2.5 %copy-start.6 = (s32[16]{0:T(128)S(1)}, s32[16]{0:T(128)}, u32[]{:S(2)}) copy-start(s32[16]{0:T(128)} %param.12) | copy-start | bytes 196
  13.5 5.5 %collective-permute-start.9 = (f32[128,128]{1,0:T(8,128)S(1)}, f32[128,128]{1,0:T(8,128)S(1)}, u32[]{:S(2)}, u32[]{:S(2)}) collective-permute-start(f32[128,128]{1,0:T(8,128)S(1)} %pad_maximum_fusion.1), channel_id=1, source_target_pairs={{0,2},{1,3},{2,0},{3,1},{4,6},{5,7},{6,4},{7,5},{8,10},{9,11},{10,... | collective-permute-start | bytes 196616 | tf_op jit(solution)/shard_map/ppermute | solution.py:329
  13.6 6.8 %collective-permute-start.10 = (f32[512,128]{1,0:T(8,128)S(1)}, f32[512,128]{1,0:T(8,128)S(1)}, u32[]{:S(2)}, u32[]{:S(2)}) collective-permute-start(f32[512,128]{1,0:T(8,128)S(1)} %bitcast.18), channel_id=1, source_target_pairs={{1,0},{2,1},{3,2},{4,3},{5,4},{6,5},{7,6},{8,7},{9,8},{10,9},{11,1... | collective-permute-start | bytes 786440 | tf_op jit(solution)/shard_map/ppermute | solution.py:362
  16.0 1.2 %copy-start.1 = (f32[16,128,128]{2,1,0:T(8,128)S(1)}, f32[16,128,128]{2,1,0:T(8,128)}, u32[]{:S(2)}) copy-start(f32[16,128,128]{2,1,0:T(8,128)} %patterns_ref) | copy-start | bytes 3145732
  17.2 1.1 %copy-start.2 = (f32[12,128,128]{2,1,0:T(8,128)S(1)}, f32[12,128,128]{2,1,0:T(8,128)}, u32[]{:S(2)}) copy-start(f32[12,128,128]{2,1,0:T(8,128)} %constant.7.clone.factors_ref) | copy-start | bytes 2359300
  19.0 1.4 %collective-permute-start.11 = (f32[256,128]{1,0:T(8,128)S(1)}, f32[256,128]{1,0:T(8,128)S(1)}, u32[]{:S(2)}, u32[]{:S(2)}) collective-permute-start(f32[256,128]{1,0:T(8,128)S(1)} %pad_maximum_fusion.near_ref), channel_id=1, source_target_pairs={{0,1},{1,0},{2,3},{3,2},{4,5},{5,4},{6,7},{7,6},{8,9},{9,8},{10,11... | collective-permute-start | bytes 393224 | tf_op jit(solution)/shard_map/ppermute | solution.py:329
  29.4 23.1 %collective-permute-start.12 = (f32[1024,128]{1,0:T(8,128)S(1)}, f32[1024,128]{1,0:T(8,128)S(1)}, u32[]{:S(2)}, u32[]{:S(2)}) collective-permute-start(f32[1024,128]{1,0:T(8,128)S(1)} %get-tuple-element.49), channel_id=1, source_target_pairs={{0,1},{1,2},{2,3},{3,4},{4,5},{5,6},{6,7},{7,8},{8,9},{9,10},{10,1... | collective-permute-start | bytes 1572872 | tf_op jit(solution)/shard_map/ppermute | solution.py:369
  29.5 1.6 %collective-permute-start = (f32[256,128]{1,0:T(8,128)S(1)}, f32[256,128]{1,0:T(8,128)S(1)}, u32[]{:S(2)}, u32[]{:S(2)}) collective-permute-start(f32[256,128]{1,0:T(8,128)S(1)} %get-tuple-element.6), channel_id=1, source_target_pairs={{0,1},{1,0},{2,3},{3,2},{4,5},{5,4},{6,7},{7,6},{8,9},{9,8},{10,11... | collective-permute-start | bytes 393224 | tf_op jit(solution)/shard_map/cond/branch_1_fun/ppermute | solution.py:329
  31.2 13.9 %collective-permute-start.2 = (f32[64,128]{1,0:T(8,128)S(1)}, f32[64,128]{1,0:T(8,128)S(1)}, u32[]{:S(2)}, u32[]{:S(2)}) collective-permute-start(f32[64,128]{1,0:T(8,128)S(1)} %get-tuple-element.51), channel_id=1, source_target_pairs={{0,8},{1,9},{2,10},{3,11},{4,12},{5,13},{6,14},{7,15},{8,0},{9,1},... | collective-permute-start | bytes 98312 | tf_op jit(solution)/shard_map/cond/branch_1_fun/ppermute | solution.py:338
  42.9 3.9 %collective-permute-start.3 = (f32[64,128]{1,0:T(8,128)S(1)}, f32[64,128]{1,0:T(8,128)S(1)}, u32[]{:S(2)}, u32[]{:S(2)}) collective-permute-start(f32[64,128]{1,0:T(8,128)S(1)} %get-tuple-element.52), channel_id=1, source_target_pairs={{0,12},{1,13},{2,14},{3,15},{4,0},{5,1},{6,2},{7,3},{8,4},{9,5},{1... | collective-permute-start | bytes 98312 | tf_op jit(solution)/shard_map/cond/branch_1_fun/ppermute | solution.py:338
  42.9 5.7 %collective-permute-start.1 = (f32[64,128]{1,0:T(8,128)S(1)}, f32[64,128]{1,0:T(8,128)S(1)}, u32[]{:S(2)}, u32[]{:S(2)}) collective-permute-start(f32[64,128]{1,0:T(8,128)S(1)} %get-tuple-element.53), channel_id=1, source_target_pairs={{0,4},{1,5},{2,6},{3,7},{4,8},{5,9},{6,10},{7,11},{8,12},{9,13},{1... | collective-permute-start | bytes 98312 | tf_op jit(solution)/shard_map/cond/branch_1_fun/ppermute | solution.py:338
  48.6 3.8 %collective-permute-start.4 = (f32[32,128]{1,0:T(8,128)S(1)}, f32[32,128]{1,0:T(8,128)S(1)}, u32[]{:S(2)}, u32[]{:S(2)}) collective-permute-start(f32[32,128]{1,0:T(8,128)S(1)} %slice.23), channel_id=1, source_target_pairs={{0,2},{1,3},{2,0},{3,1},{4,6},{5,7},{6,4},{7,5},{8,10},{9,11},{10,... | collective-permute-start | bytes 49160 | tf_op jit(solution)/shard_map/cond/branch_1_fun/ppermute | solution.py:329
  52.4 0.9 %copy-start.3 = (f32[8,2,2,128]{3,2,1,0:T(2,128)}, f32[8,2,2,128]{3,2,1,0:T(2,128)S(1)}, u32[]{:S(2)}) copy-start(f32[8,2,2,128]{3,2,1,0:T(2,128)S(1)} %get-tuple-element.56) | copy-start | bytes 49156

commit v2 on v1

--- a/solution.py
+++ b/solution.py
@@ -229,7 +229,7 @@
     fours = lax.shift_right_logical(count, 2)
 
     def eight(j, carry):
-        run(*([8 * j + k, 8 * j + k + 1] for k in range(0, 8, 2)))
+        run(*([8 * j + k + i for i in range(4)] for k in (0, 4)))
         return carry
 
     def four(j, carry):

time: 52.4 us -> 52.4 us (level); the launches traced: 53.3 us -> 52.1 us
  Pallas kernels: 9.57 us -> 8.51 us
    ppermute x3, starting transfers between devices: 13.7 us -> 3.53 us  [places_on(): lax.ppermute(value, 'tile', [(i, i // GROUP_DEV * GROUP_DEV + (i + distan...]
    ppermute x7, starting transfers between devices: 5.19 us -> 15.3 us  [partner(): lax.ppermute(value, 'tile', [(i, i ^ bits) for i in range(lax.axis_size('...]
    ppermute x7, waiting for transfers between devices: 7.17 us -> 5.1 us  [partner(): lax.ppermute(value, 'tile', [(i, i ^ bits) for i in range(lax.axis_size('...]
    ppermute x3, waiting for transfers between devices: 3.69 us -> 5.71 us  [places_on(): lax.ppermute(value, 'tile', [(i, i // GROUP_DEV * GROUP_DEV + (i + distan...]
    pallas_call x1, Pallas kernels: 8.96 us -> 7.9 us  [terms(): pl.pallas_call(kernel, out_shape=(jax.ShapeDtypeStruct((planes.shape[1] *...]
  transfers between devices with their start and end apart: 13 -> 13, of which waited for: 8 -> 7; matrix products, arithmetic and copies ran while one was open for 0% -> 0% of each run, Pallas kernels for 1% -> 1%
where the time goes in v2:
time: 52.4 us; the launch traced here: 52.1 us
  starting transfers between devices  26.7 us (51%)
  waiting for transfers between devices  10.8 us (21%)
  Pallas kernels  8.51 us (16%)
  local copies, waits for them, and re-layouts  3.62 us (7%)
  between operations  1.4 us (3%)
  other arithmetic  0.97 us (2%)
    ppermute x7, starting transfers between devices, partner(): lax.ppermute(value, 'tile', [(i, i ^ bits) for i in range(lax.axis_size('...  15.3 us
    pallas_call x1, Pallas kernels, terms(): pl.pallas_call(kernel, out_shape=(jax.ShapeDtypeStruct((planes.shape[1] *...  7.9 us
    ppermute x3, waiting for transfers between devices, places_on(): lax.ppermute(value, 'tile', [(i, i // GROUP_DEV * GROUP_DEV + (i + distan...  5.71 us
    ppermute x1, starting transfers between devices, shards(): low = lax.ppermute(low, 'tile', down)  5.47 us
    ppermute x7, waiting for transfers between devices, partner(): lax.ppermute(value, 'tile', [(i, i ^ bits) for i in range(lax.axis_size('...  5.1 us
    ppermute x3, starting transfers between devices, places_on(): lax.ppermute(value, 'tile', [(i, i // GROUP_DEV * GROUP_DEV + (i + distan...  3.53 us
    unnamed x14, local copies, waits for them, and re-layouts  2.38 us
    ppermute x1, starting transfers between devices, shards(): high = lax.ppermute(high, 'tile', down)  2.36 us
  transfers between devices with their start and end apart: 13, of which 7 were waited for; matrix products, arithmetic and copies ran while one was open for 0% of the time, Pallas kernels for 1%

profile of v2, /device:TPU:0, one launch (start us, length us, event | category | flops | bytes accessed | tf_op | source)
XLA Modules:
  0.0 52.1 jit_solution(774469686864396466)
XLA Ops:
  0.6 0.0 copy-start.4
  0.6 0.0 copy-start
  0.6 1.2 %fusion.1 = (f32[64,2,2,2,128]{4,3,2,1,0:T(2,128)S(1)}, f32[64,2,2,2,128]{4,3,2,1,0:T(2,128)S(1)}) fusion(f32[128,2,2,2,128]{4,3,2,1,0:T(2,128)} %bitcast.15), kind=kLoop, calls=%fused_computation.6 | loop fusion | bytes 1048576 | tf_op jit(solution)/shard_map/slice | solution.py:333
  1.9 5.5 %collective-permute-start.5 = (f32[512,128]{1,0:T(8,128)S(1)}, f32[512,128]{1,0:T(8,128)S(1)}, u32[]{:S(2)}, u32[]{:S(2)}) collective-permute-start(f32[512,128]{1,0:T(8,128)S(1)} %bitcast.19), channel_id=1, source_target_pairs={{1,0},{2,1},{3,2},{4,3},{5,4},{6,5},{7,6},{8,7},{9,8},{10,9},{11,1... | collective-permute-start | bytes 786440 | tf_op jit(solution)/shard_map/ppermute | solution.py:358
  7.3 0.0 copy-done.4
  7.3 0.4 collective-permute-start.8
  7.8 0.0 collective-permute-start.7
  7.8 3.9 %collective-permute-start.6 = (f32[32,128]{1,0:T(8,128)S(1)}, f32[32,128]{1,0:T(8,128)S(1)}, u32[]{:S(2)}, u32[]{:S(2)}) collective-permute-start(f32[32,128]{1,0:T(8,128)S(1)} %bitcast.23), channel_id=1, source_target_pairs={{0,8},{1,9},{2,10},{3,11},{4,12},{5,13},{6,14},{7,15},{8,0},{9,1},... | collective-permute-start | bytes 49160 | tf_op jit(solution)/shard_map/ppermute | solution.py:329
  12.4 0.5 collective-permute-done.8
  12.9 0.0 collective-permute-done.7
  12.9 0.6 %collective-permute-done.6 = f32[32,128]{1,0:T(8,128)S(1)} collective-permute-done((f32[32,128]{1,0:T(8,128)S(1)}, f32[32,128]{1,0:T(8,128)S(1)}, u32[]{:S(2)}, u32[]{:S(2)}) %collective-permute-start.6) | collective-permute-done | bytes 16416 | tf_op jit(solution)/shard_map/ppermute | solution.py:329
  13.5 0.0 copy-start.5
  13.5 0.0 copy-start.6
  13.5 0.0 collective-permute-done.5.low_ref
  13.5 0.1 collective-permute-start.9
  13.6 2.4 %collective-permute-start.10 = (f32[512,128]{1,0:T(8,128)S(1)}, f32[512,128]{1,0:T(8,128)S(1)}, u32[]{:S(2)}, u32[]{:S(2)}) collective-permute-start(f32[512,128]{1,0:T(8,128)S(1)} %bitcast.18), channel_id=1, source_target_pairs={{1,0},{2,1},{3,2},{4,3},{5,4},{6,5},{7,6},{8,7},{9,8},{10,9},{11,1... | collective-permute-start | bytes 786440 | tf_op jit(solution)/shard_map/ppermute | solution.py:362
  15.9 0.0 copy-done.5
  15.9 0.0 copy-done.6
  15.9 0.1 pad_add_fusion.scalars_ref
  16.0 0.0 copy-done
  16.0 0.0 copy-start.1
  16.0 1.2 %copy-done.1 = f32[16,128,128]{2,1,0:T(8,128)S(1)} copy-done((f32[16,128,128]{2,1,0:T(8,128)S(1)}, f32[16,128,128]{2,1,0:T(8,128)}, u32[]{:S(2)}) %copy-start.1) | copy-done | bytes 1048600
  17.2 0.0 copy-start.2
  17.2 1.1 %copy-done.2 = f32[12,128,128]{2,1,0:T(8,128)S(1)} copy-done((f32[12,128,128]{2,1,0:T(8,128)S(1)}, f32[12,128,128]{2,1,0:T(8,128)}, u32[]{:S(2)}) %copy-start.2) | copy-done | bytes 786456
  18.4 0.6 %shard_map.86 = (f32[8,128,128]{2,1,0:T(8,128)S(1)}, f32[16,128,128]{2,1,0:T(8,128)S(1)}, bf16[8,256,256]{2,1,0:T(8,128)(2,1)S(1)}, bf16[8,256,256]{2,1,0:T(8,128)(2,1)S(1)}) custom-call(f32[1024,128]{1,0:T(8,128)S(1)} %bitcast.16, f32[16,128,128]{2,1,0:T(8,128)S(1)} %copy-done.1, f32[12,128,128]{2,1,0:T(8,128)S(1)} %copy-done.2), custom_call_target="tpu_custom_call" | custom-call | bytes 6291456 | tf_op jit(solution)/shard_map/pallas_call | solution.py:263
  18.9 0.0 collective-permute-done.9
  19.0 0.1 collective-permute-start.11
  19.0 1.3 %collective-permute-done.11.far_ref = f32[256,128]{1,0:T(8,128)S(1)} collective-permute-done((f32[256,128]{1,0:T(8,128)S(1)}, f32[256,128]{1,0:T(8,128)S(1)}, u32[]{:S(2)}, u32[]{:S(2)}) %collective-permute-start.11) | collective-permute-done | bytes 131104 | tf_op jit(solution)/shard_map/ppermute | solution.py:329
  20.4 0.0 collective-permute-done.10.high_ref
  20.4 7.9 %shard_map.87 = (f32[1024,128]{1,0:T(8,128)S(1)}, f32[1024,128]{1,0:T(8,128)S(1)}, f32[4,128,128]{2,1,0:T(8,128)S(1)}) custom-call(s32[33]{0:T(128)S(1)} %pad_add_fusion.scalars_ref, f32[8,128,128]{2,1,0:T(8,128)S(1)} %get-tuple-element.41.own_ref, f32[512,128]{1,0:T(8,128)S(1)} %collective-permute-done.5.low_ref, ...), custom_call_target="tpu_custom_call" | custom-call | tf_op jit(solution)/shard_map/pallas_call | solution.py:288
  28.3 0.1 collective-permute-start.12
  28.4 22.9 %conditional.1 = (f32[8,2,2,128]{3,2,1,0:T(2,128)S(1)}) conditional(s32[]{:T(128)} %bitcast.11, () %tuple.22, f32[4,128,128]{2,1,0:T(8,128)S(1)} %get-tuple-element.50), branch_computations={%region_0.0_spmd, %region_1.0_spmd} | conditional | flops 61440 | bytes 1818832 | solution.py:370
  28.4 2.7 %collective-permute-start = (f32[256,128]{1,0:T(8,128)S(1)}, f32[256,128]{1,0:T(8,128)S(1)}, u32[]{:S(2)}, u32[]{:S(2)}) collective-permute-start(f32[256,128]{1,0:T(8,128)S(1)} %get-tuple-element.6), channel_id=1, source_target_pairs={{0,1},{1,0},{2,3},{3,2},{4,5},{5,4},{6,7},{7,6},{8,9},{9,8},{10,11... | collective-permute-start | bytes 393224 | tf_op jit(solution)/shard_map/cond/branch_1_fun/ppermute | solution.py:329
  31.1 1.0 %collective-permute-done = f32[256,128]{1,0:T(8,128)S(1)} collective-permute-done((f32[256,128]{1,0:T(8,128)S(1)}, f32[256,128]{1,0:T(8,128)S(1)}, u32[]{:S(2)}, u32[]{:S(2)}) %collective-permute-start) | collective-permute-done | bytes 131104 | tf_op jit(solution)/shard_map/cond/branch_1_fun/ppermute | solution.py:329
  32.1 0.1 collective-permute-start.2
  32.2 3.5 %collective-permute-start.3 = (f32[64,128]{1,0:T(8,128)S(1)}, f32[64,128]{1,0:T(8,128)S(1)}, u32[]{:S(2)}, u32[]{:S(2)}) collective-permute-start(f32[64,128]{1,0:T(8,128)S(1)} %get-tuple-element.52), channel_id=1, source_target_pairs={{0,12},{1,13},{2,14},{3,15},{4,0},{5,1},{6,2},{7,3},{8,4},{9,5},{1... | collective-permute-start | bytes 98312 | tf_op jit(solution)/shard_map/cond/branch_1_fun/ppermute | solution.py:338
  35.7 0.0 collective-permute-start.1
  35.7 2.0 %collective-permute-done.2 = f32[64,128]{1,0:T(8,128)S(1)} collective-permute-done((f32[64,128]{1,0:T(8,128)S(1)}, f32[64,128]{1,0:T(8,128)S(1)}, u32[]{:S(2)}, u32[]{:S(2)}) %collective-permute-start.2) | collective-permute-done | bytes 32800 | tf_op jit(solution)/shard_map/cond/branch_1_fun/ppermute | solution.py:338
  37.7 0.0 collective-permute-done.3
  37.7 3.7 %collective-permute-done.1 = f32[64,128]{1,0:T(8,128)S(1)} collective-permute-done((f32[64,128]{1,0:T(8,128)S(1)}, f32[64,128]{1,0:T(8,128)S(1)}, u32[]{:S(2)}, u32[]{:S(2)}) %collective-permute-start.1) | collective-permute-done | bytes 32800 | tf_op jit(solution)/shard_map/cond/branch_1_fun/ppermute | solution.py:338
  41.4 8.1 %collective-permute-start.4 = (f32[32,128]{1,0:T(8,128)S(1)}, f32[32,128]{1,0:T(8,128)S(1)}, u32[]{:S(2)}, u32[]{:S(2)}) collective-permute-start(f32[32,128]{1,0:T(8,128)S(1)} %slice.23), channel_id=1, source_target_pairs={{0,2},{1,3},{2,0},{3,1},{4,6},{5,7},{6,4},{7,5},{8,10},{9,11},{10,... | collective-permute-start | bytes 49160 | tf_op jit(solution)/shard_map/cond/branch_1_fun/ppermute | solution.py:329
  49.5 1.7 %collective-permute-done.4 = f32[32,128]{1,0:T(8,128)S(1)} collective-permute-done((f32[32,128]{1,0:T(8,128)S(1)}, f32[32,128]{1,0:T(8,128)S(1)}, u32[]{:S(2)}, u32[]{:S(2)}) %collective-permute-start.4) | collective-permute-done | bytes 16416 | tf_op jit(solution)/shard_map/cond/branch_1_fun/ppermute | solution.py:329
  51.2 0.0 copy-start.3
  51.2 0.0 collective-permute-done.12
  51.2 0.8 %add.18 = f32[1024,128]{1,0:T(8,128)} add(f32[1024,128]{1,0:T(8,128)S(1)} %get-tuple-element.48, f32[1024,128]{1,0:T(8,128)S(1)} %collective-permute-done.12) | non-fusion elementwise | flops 131072 | bytes 1572864 | tf_op jit(solution)/shard_map/add | solution.py:375
  52.1 0.0 copy-done.3
  (8 shorter events, 0.1 us)
Async XLA Ops:
  0.6 6.7 %copy-start.4 = (f32[8,2,2,128]{3,2,1,0:T(2,128)S(1)}, f32[8,2,2,128]{3,2,1,0:T(2,128)}, u32[]{:S(2)}) copy-start(f32[8,2,2,128]{3,2,1,0:T(2,128)} %param.10) | copy-start | bytes 49156
  0.6 15.4 %copy-start = (f32[128,2,2,256]{3,2,1,0:T(2,128)S(1)}, f32[128,2,2,256]{3,2,1,0:T(2,128)}, u32[]{:S(2)}) copy-start(f32[128,2,2,256]{3,2,1,0:T(2,128)} %param.9) | copy-start | bytes 1572868
  1.9 11.6 %collective-permute-start.5 = (f32[512,128]{1,0:T(8,128)S(1)}, f32[512,128]{1,0:T(8,128)S(1)}, u32[]{:S(2)}, u32[]{:S(2)}) collective-permute-start(f32[512,128]{1,0:T(8,128)S(1)} %bitcast.19), channel_id=1, source_target_pairs={{1,0},{2,1},{3,2},{4,3},{5,4},{6,5},{7,6},{8,7},{9,8},{10,9},{11,1... | collective-permute-start | bytes 786440 | tf_op jit(solution)/shard_map/ppermute | solution.py:358
  7.3 5.5 %collective-permute-start.8 = (f32[32,128]{1,0:T(8,128)S(1)}, f32[32,128]{1,0:T(8,128)S(1)}, u32[]{:S(2)}, u32[]{:S(2)}) collective-permute-start(f32[32,128]{1,0:T(8,128)S(1)} %bitcast.21), channel_id=1, source_target_pairs={{0,12},{1,13},{2,14},{3,15},{4,8},{5,9},{6,10},{7,11},{8,4},{9,5},... | collective-permute-start | bytes 49160 | tf_op jit(solution)/shard_map/ppermute | solution.py:329
  7.8 5.1 %collective-permute-start.7 = (f32[32,128]{1,0:T(8,128)S(1)}, f32[32,128]{1,0:T(8,128)S(1)}, u32[]{:S(2)}, u32[]{:S(2)}) collective-permute-start(f32[32,128]{1,0:T(8,128)S(1)} %bitcast.22), channel_id=1, source_target_pairs={{0,4},{1,5},{2,6},{3,7},{4,0},{5,1},{6,2},{7,3},{8,12},{9,13},{10,... | collective-permute-start | bytes 49160 | tf_op jit(solution)/shard_map/ppermute | solution.py:329
  7.8 5.7 %collective-permute-start.6 = (f32[32,128]{1,0:T(8,128)S(1)}, f32[32,128]{1,0:T(8,128)S(1)}, u32[]{:S(2)}, u32[]{:S(2)}) collective-permute-start(f32[32,128]{1,0:T(8,128)S(1)} %bitcast.23), channel_id=1, source_target_pairs={{0,8},{1,9},{2,10},{3,11},{4,12},{5,13},{6,14},{7,15},{8,0},{9,1},... | collective-permute-start | bytes 49160 | tf_op jit(solution)/shard_map/ppermute | solution.py:329
  13.5 2.5 %copy-start.5 = (s32[16]{0:T(128)S(1)}, s32[16]{0:T(128)}, u32[]{:S(2)}) copy-start(s32[16]{0:T(128)} %param.13) | copy-start | bytes 196
  13.5 2.5 %copy-start.6 = (s32[16]{0:T(128)S(1)}, s32[16]{0:T(128)}, u32[]{:S(2)}) copy-start(s32[16]{0:T(128)} %param.12) | copy-start | bytes 196
  13.5 5.5 %collective-permute-start.9 = (f32[128,128]{1,0:T(8,128)S(1)}, f32[128,128]{1,0:T(8,128)S(1)}, u32[]{:S(2)}, u32[]{:S(2)}) collective-permute-start(f32[128,128]{1,0:T(8,128)S(1)} %pad_maximum_fusion.1), channel_id=1, source_target_pairs={{0,2},{1,3},{2,0},{3,1},{4,6},{5,7},{6,4},{7,5},{8,10},{9,11},{10,... | collective-permute-start | bytes 196616 | tf_op jit(solution)/shard_map/ppermute | solution.py:329
  13.6 6.8 %collective-permute-start.10 = (f32[512,128]{1,0:T(8,128)S(1)}, f32[512,128]{1,0:T(8,128)S(1)}, u32[]{:S(2)}, u32[]{:S(2)}) collective-permute-start(f32[512,128]{1,0:T(8,128)S(1)} %bitcast.18), channel_id=1, source_target_pairs={{1,0},{2,1},{3,2},{4,3},{5,4},{6,5},{7,6},{8,7},{9,8},{10,9},{11,1... | collective-permute-start | bytes 786440 | tf_op jit(solution)/shard_map/ppermute | solution.py:362
  16.0 1.2 %copy-start.1 = (f32[16,128,128]{2,1,0:T(8,128)S(1)}, f32[16,128,128]{2,1,0:T(8,128)}, u32[]{:S(2)}) copy-start(f32[16,128,128]{2,1,0:T(8,128)} %patterns_ref) | copy-start | bytes 3145732
  17.2 1.1 %copy-start.2 = (f32[12,128,128]{2,1,0:T(8,128)S(1)}, f32[12,128,128]{2,1,0:T(8,128)}, u32[]{:S(2)}) copy-start(f32[12,128,128]{2,1,0:T(8,128)} %constant.7.clone.factors_ref) | copy-start | bytes 2359300
  19.0 1.4 %collective-permute-start.11 = (f32[256,128]{1,0:T(8,128)S(1)}, f32[256,128]{1,0:T(8,128)S(1)}, u32[]{:S(2)}, u32[]{:S(2)}) collective-permute-start(f32[256,128]{1,0:T(8,128)S(1)} %pad_maximum_fusion.near_ref), channel_id=1, source_target_pairs={{0,1},{1,0},{2,3},{3,2},{4,5},{5,4},{6,7},{7,6},{8,9},{9,8},{10,11... | collective-permute-start | bytes 393224 | tf_op jit(solution)/shard_map/ppermute | solution.py:329
  28.3 22.9 %collective-permute-start.12 = (f32[1024,128]{1,0:T(8,128)S(1)}, f32[1024,128]{1,0:T(8,128)S(1)}, u32[]{:S(2)}, u32[]{:S(2)}) collective-permute-start(f32[1024,128]{1,0:T(8,128)S(1)} %get-tuple-element.49), channel_id=1, source_target_pairs={{0,1},{1,2},{2,3},{3,4},{4,5},{5,6},{6,7},{7,8},{8,9},{9,10},{10,1... | collective-permute-start | bytes 1572872 | tf_op jit(solution)/shard_map/ppermute | solution.py:369
  28.4 3.6 %collective-permute-start = (f32[256,128]{1,0:T(8,128)S(1)}, f32[256,128]{1,0:T(8,128)S(1)}, u32[]{:S(2)}, u32[]{:S(2)}) collective-permute-start(f32[256,128]{1,0:T(8,128)S(1)} %get-tuple-element.6), channel_id=1, source_target_pairs={{0,1},{1,0},{2,3},{3,2},{4,5},{5,4},{6,7},{7,6},{8,9},{9,8},{10,11... | collective-permute-start | bytes 393224 | tf_op jit(solution)/shard_map/cond/branch_1_fun/ppermute | solution.py:329
  32.1 5.6 %collective-permute-start.2 = (f32[64,128]{1,0:T(8,128)S(1)}, f32[64,128]{1,0:T(8,128)S(1)}, u32[]{:S(2)}, u32[]{:S(2)}) collective-permute-start(f32[64,128]{1,0:T(8,128)S(1)} %get-tuple-element.51), channel_id=1, source_target_pairs={{0,8},{1,9},{2,10},{3,11},{4,12},{5,13},{6,14},{7,15},{8,0},{9,1},... | collective-permute-start | bytes 98312 | tf_op jit(solution)/shard_map/cond/branch_1_fun/ppermute | solution.py:338
  32.2 5.5 %collective-permute-start.3 = (f32[64,128]{1,0:T(8,128)S(1)}, f32[64,128]{1,0:T(8,128)S(1)}, u32[]{:S(2)}, u32[]{:S(2)}) collective-permute-start(f32[64,128]{1,0:T(8,128)S(1)} %get-tuple-element.52), channel_id=1, source_target_pairs={{0,12},{1,13},{2,14},{3,15},{4,0},{5,1},{6,2},{7,3},{8,4},{9,5},{1... | collective-permute-start | bytes 98312 | tf_op jit(solution)/shard_map/cond/branch_1_fun/ppermute | solution.py:338
  35.7 5.7 %collective-permute-start.1 = (f32[64,128]{1,0:T(8,128)S(1)}, f32[64,128]{1,0:T(8,128)S(1)}, u32[]{:S(2)}, u32[]{:S(2)}) collective-permute-start(f32[64,128]{1,0:T(8,128)S(1)} %get-tuple-element.53), channel_id=1, source_target_pairs={{0,4},{1,5},{2,6},{3,7},{4,8},{5,9},{6,10},{7,11},{8,12},{9,13},{1... | collective-permute-start | bytes 98312 | tf_op jit(solution)/shard_map/cond/branch_1_fun/ppermute | solution.py:338
  41.4 9.8 %collective-permute-start.4 = (f32[32,128]{1,0:T(8,128)S(1)}, f32[32,128]{1,0:T(8,128)S(1)}, u32[]{:S(2)}, u32[]{:S(2)}) collective-permute-start(f32[32,128]{1,0:T(8,128)S(1)} %slice.23), channel_id=1, source_target_pairs={{0,2},{1,3},{2,0},{3,1},{4,6},{5,7},{6,4},{7,5},{8,10},{9,11},{10,... | collective-permute-start | bytes 49160 | tf_op jit(solution)/shard_map/cond/branch_1_fun/ppermute | solution.py:329
  51.2 0.9 %copy-start.3 = (f32[8,2,2,128]{3,2,1,0:T(2,128)}, f32[8,2,2,128]{3,2,1,0:T(2,128)S(1)}, u32[]{:S(2)}) copy-start(f32[8,2,2,128]{3,2,1,0:T(2,128)S(1)} %get-tuple-element.56) | copy-start | bytes 49156

commit v3 on v2

--- a/solution.py
+++ b/solution.py
@@ -357,11 +357,11 @@
     low, high, mine = lax.optimization_barrier((low, high, flat(probe_field)))
     low = lax.ppermute(low, "tile", down)
     quarter = jnp.concatenate([mine, partner(mine, 8), partner(mine, 4), partner(mine, 12)], axis=0)
-    low, high, quarter, patterns, own = lax.optimization_barrier((low, high, quarter, patterns, own))
+    planes, patterns, *mats = prepared(own, patterns)
+    low, high, quarter, planes, patterns, scalars, *mats = lax.optimization_barrier(
+        (low, high, quarter, planes, patterns, scalars, *mats))
     near = jnp.concatenate([quarter, partner(quarter, 2)], axis=0)
     high = lax.ppermute(high, "tile", down)
-    planes, patterns, *mats = prepared(own, patterns)
-    near, planes, patterns, scalars, *mats = lax.optimization_barrier((near, planes, patterns, scalars, *mats))
     far = partner(near, 1)
 
     own_grad, back, probe_grad = terms(scalars, planes, low, high, near, far, patterns, mats)

time: 52.4 us -> 52.1 us (level)
  starting transfers between devices: 26.7 us -> 21.5 us
  Pallas kernels: 8.51 us -> 11.3 us
  waiting for transfers between devices: 10.8 us -> 12.5 us
    ppermute x7, waiting for transfers between devices: 5.1 us -> 7.92 us  [partner(): lax.ppermute(value, 'tile', [(i, i ^ bits) for i in range(lax.axis_size('...]
    pallas_call x1, Pallas kernels: 7.9 us -> 10.7 us  [terms(): pl.pallas_call(kernel, out_shape=(jax.ShapeDtypeStruct((planes.shape[1] *...]
    ppermute x1, starting transfers between devices: 2.36 us -> 0.38 us  [shards(): high = lax.ppermute(high, 'tile', down)]
    ppermute x7, starting transfers between devices: 15.3 us -> 13.5 us  [partner(): lax.ppermute(value, 'tile', [(i, i ^ bits) for i in range(lax.axis_size('...]
    ppermute x3, starting transfers between devices: 3.53 us -> 2.16 us  [places_on(): lax.ppermute(value, 'tile', [(i, i // GROUP_DEV * GROUP_DEV + (i + distan...]
    ppermute x3, waiting for transfers between devices: 5.71 us -> 4.53 us  [places_on(): lax.ppermute(value, 'tile', [(i, i // GROUP_DEV * GROUP_DEV + (i + distan...]
    unnamed x14 -> x15, local copies, waits for them, and re-layouts: 2.38 us -> 2.39 us
  transfers between devices with their start and end apart: 13 -> 13, of which waited for: 7 -> 6; matrix products, arithmetic and copies ran while one was open for 0% -> 0% of each run, Pallas kernels for 1% -> 1%
where the time goes in v3:
time: 52.1 us; the launch traced here: 51.4 us
  starting transfers between devices  21.5 us (41%)
  waiting for transfers between devices  12.5 us (24%)
  Pallas kernels  11.3 us (22%)
  local copies, waits for them, and re-layouts  3.63 us (7%)
  between operations  1.43 us (3%)
  other arithmetic  0.96 us (2%)
    ppermute x7, starting transfers between devices, partner(): lax.ppermute(value, 'tile', [(i, i ^ bits) for i in range(lax.axis_size('...  13.5 us
    pallas_call x1, Pallas kernels, terms(): pl.pallas_call(kernel, out_shape=(jax.ShapeDtypeStruct((planes.shape[1] *...  10.7 us
    ppermute x7, waiting for transfers between devices, partner(): lax.ppermute(value, 'tile', [(i, i ^ bits) for i in range(lax.axis_size('...  7.92 us
    ppermute x1, starting transfers between devices, shards(): low = lax.ppermute(low, 'tile', down)  5.47 us
    ppermute x3, waiting for transfers between devices, places_on(): lax.ppermute(value, 'tile', [(i, i // GROUP_DEV * GROUP_DEV + (i + distan...  4.53 us
    unnamed x15, local copies, waits for them, and re-layouts  2.39 us
    ppermute x3, starting transfers between devices, places_on(): lax.ppermute(value, 'tile', [(i, i // GROUP_DEV * GROUP_DEV + (i + distan...  2.16 us
    slice x2, local copies, waits for them, and re-layouts, halved(): return (value[:value.shape[0] // 2], value[value.shape[0] // 2:])  1.23 us
  transfers between devices with their start and end apart: 13, of which 6 were waited for; matrix products, arithmetic and copies ran while one was open for 0% of the time, Pallas kernels for 1%

profile of v3, /device:TPU:0, one launch (start us, length us, event | category | flops | bytes accessed | tf_op | source)
XLA Modules:
  0.0 51.4 jit_solution(8095146586289218317)
XLA Ops:
  0.6 0.0 copy-start.4
  0.6 0.0 copy-start
  0.6 1.2 %fusion.1 = (f32[64,2,2,2,128]{4,3,2,1,0:T(2,128)S(1)}, f32[64,2,2,2,128]{4,3,2,1,0:T(2,128)S(1)}) fusion(f32[128,2,2,2,128]{4,3,2,1,0:T(2,128)} %bitcast.15), kind=kLoop, calls=%fused_computation.7 | loop fusion | bytes 1048576 | tf_op jit(solution)/shard_map/slice | solution.py:333
  1.9 0.0 copy-start.5
  1.9 0.0 copy-start.6
  1.9 5.5 %collective-permute-start.5 = (f32[512,128]{1,0:T(8,128)S(1)}, f32[512,128]{1,0:T(8,128)S(1)}, u32[]{:S(2)}, u32[]{:S(2)}) collective-permute-start(f32[512,128]{1,0:T(8,128)S(1)} %bitcast.19), channel_id=1, source_target_pairs={{1,0},{2,1},{3,2},{4,3},{5,4},{6,5},{7,6},{8,7},{9,8},{10,9},{11,1... | collective-permute-start | bytes 786440 | tf_op jit(solution)/shard_map/ppermute | solution.py:358
  7.4 0.0 copy-done.4
  7.4 0.4 collective-permute-start.8
  7.8 0.0 collective-permute-start.7
  7.8 3.9 %collective-permute-start.6 = (f32[32,128]{1,0:T(8,128)S(1)}, f32[32,128]{1,0:T(8,128)S(1)}, u32[]{:S(2)}, u32[]{:S(2)}) collective-permute-start(f32[32,128]{1,0:T(8,128)S(1)} %bitcast.23), channel_id=1, source_target_pairs={{0,8},{1,9},{2,10},{3,11},{4,12},{5,13},{6,14},{7,15},{8,0},{9,1},... | collective-permute-start | bytes 49160 | tf_op jit(solution)/shard_map/ppermute | solution.py:329
  12.4 0.0 copy-done.5
  12.4 0.0 copy-done.6
  12.4 0.1 pad_add_fusion.scalars_ref
  12.5 0.0 copy-done
  12.5 0.0 copy-start.1
  12.5 1.2 %copy-done.1 = f32[16,128,128]{2,1,0:T(8,128)S(1)} copy-done((f32[16,128,128]{2,1,0:T(8,128)S(1)}, f32[16,128,128]{2,1,0:T(8,128)}, u32[]{:S(2)}) %copy-start.1) | copy-done | bytes 1048600
  13.7 0.0 copy-start.2
  13.7 1.1 %copy-done.2 = f32[12,128,128]{2,1,0:T(8,128)S(1)} copy-done((f32[12,128,128]{2,1,0:T(8,128)S(1)}, f32[12,128,128]{2,1,0:T(8,128)}, u32[]{:S(2)}) %copy-start.2) | copy-done | bytes 786456
  14.9 0.6 %shard_map.86 = (f32[8,128,128]{2,1,0:T(8,128)S(1)}, f32[16,128,128]{2,1,0:T(8,128)S(1)}, bf16[8,256,256]{2,1,0:T(8,128)(2,1)S(1)}, bf16[8,256,256]{2,1,0:T(8,128)(2,1)S(1)}) custom-call(f32[1024,128]{1,0:T(8,128)S(1)} %bitcast.16, f32[16,128,128]{2,1,0:T(8,128)S(1)} %copy-done.1, f32[12,128,128]{2,1,0:T(8,128)S(1)} %copy-done.2), custom_call_target="tpu_custom_call" | custom-call | bytes 6291456 | tf_op jit(solution)/shard_map/pallas_call | solution.py:263
  15.4 0.0 collective-permute-done.8
  15.4 0.0 collective-permute-done.7
  15.5 0.0 collective-permute-done.6
  15.5 0.0 collective-permute-done.5.low_ref
  15.5 0.1 collective-permute-start.10
  15.6 0.4 collective-permute-start.9
  16.0 3.9 %collective-permute-done.10 = f32[128,128]{1,0:T(8,128)S(1)} collective-permute-done((f32[128,128]{1,0:T(8,128)S(1)}, f32[128,128]{1,0:T(8,128)S(1)}, u32[]{:S(2)}, u32[]{:S(2)}) %collective-permute-start.10) | collective-permute-done | bytes 65568 | tf_op jit(solution)/shard_map/ppermute | solution.py:329
  19.8 0.0 collective-permute-start.11
  19.8 1.3 %collective-permute-done.11.far_ref = f32[256,128]{1,0:T(8,128)S(1)} collective-permute-done((f32[256,128]{1,0:T(8,128)S(1)}, f32[256,128]{1,0:T(8,128)S(1)}, u32[]{:S(2)}, u32[]{:S(2)}) %collective-permute-start.11) | collective-permute-done | bytes 131104 | tf_op jit(solution)/shard_map/ppermute | solution.py:329
  21.2 0.0 collective-permute-done.9.high_ref
  21.2 10.7 %shard_map.87 = (f32[1024,128]{1,0:T(8,128)S(1)}, f32[1024,128]{1,0:T(8,128)S(1)}, f32[4,128,128]{2,1,0:T(8,128)S(1)}) custom-call(s32[33]{0:T(128)S(1)} %pad_add_fusion.scalars_ref, f32[8,128,128]{2,1,0:T(8,128)S(1)} %get-tuple-element.35.own_ref, f32[512,128]{1,0:T(8,128)S(1)} %collective-permute-done.5.low_ref, ...), custom_call_target="tpu_custom_call" | custom-call | tf_op jit(solution)/shard_map/pallas_call | solution.py:288
  31.9 0.1 collective-permute-start.12
  32.0 18.6 %conditional.1 = (f32[8,2,2,128]{3,2,1,0:T(2,128)S(1)}) conditional(s32[]{:T(128)} %bitcast.11, () %tuple.20, f32[4,128,128]{2,1,0:T(8,128)S(1)} %get-tuple-element.44), branch_computations={%region_0.0_spmd, %region_1.0_spmd} | conditional | flops 61440 | bytes 1818832 | solution.py:370
  32.0 2.4 %collective-permute-start = (f32[256,128]{1,0:T(8,128)S(1)}, f32[256,128]{1,0:T(8,128)S(1)}, u32[]{:S(2)}, u32[]{:S(2)}) collective-permute-start(f32[256,128]{1,0:T(8,128)S(1)} %get-tuple-element.6), channel_id=1, source_target_pairs={{0,1},{1,0},{2,3},{3,2},{4,5},{5,4},{6,7},{7,6},{8,9},{9,8},{10,11... | collective-permute-start | bytes 393224 | tf_op jit(solution)/shard_map/cond/branch_1_fun/ppermute | solution.py:329
  34.4 1.0 %collective-permute-done = f32[256,128]{1,0:T(8,128)S(1)} collective-permute-done((f32[256,128]{1,0:T(8,128)S(1)}, f32[256,128]{1,0:T(8,128)S(1)}, u32[]{:S(2)}, u32[]{:S(2)}) %collective-permute-start) | collective-permute-done | bytes 131104 | tf_op jit(solution)/shard_map/cond/branch_1_fun/ppermute | solution.py:329
  35.4 0.1 collective-permute-start.2
  35.5 0.1 collective-permute-start.3
  35.6 2.0 %collective-permute-start.1 = (f32[64,128]{1,0:T(8,128)S(1)}, f32[64,128]{1,0:T(8,128)S(1)}, u32[]{:S(2)}, u32[]{:S(2)}) collective-permute-start(f32[64,128]{1,0:T(8,128)S(1)} %get-tuple-element.47), channel_id=1, source_target_pairs={{0,4},{1,5},{2,6},{3,7},{4,8},{5,9},{6,10},{7,11},{8,12},{9,13},{1... | collective-permute-start | bytes 98312 | tf_op jit(solution)/shard_map/cond/branch_1_fun/ppermute | solution.py:338
  37.6 2.8 %collective-permute-done.2 = f32[64,128]{1,0:T(8,128)S(1)} collective-permute-done((f32[64,128]{1,0:T(8,128)S(1)}, f32[64,128]{1,0:T(8,128)S(1)}, u32[]{:S(2)}, u32[]{:S(2)}) %collective-permute-start.2) | collective-permute-done | bytes 32800 | tf_op jit(solution)/shard_map/cond/branch_1_fun/ppermute | solution.py:338
  40.4 0.0 collective-permute-done.3
  40.4 1.7 %collective-permute-done.1 = f32[64,128]{1,0:T(8,128)S(1)} collective-permute-done((f32[64,128]{1,0:T(8,128)S(1)}, f32[64,128]{1,0:T(8,128)S(1)}, u32[]{:S(2)}, u32[]{:S(2)}) %collective-permute-start.1) | collective-permute-done | bytes 32800 | tf_op jit(solution)/shard_map/cond/branch_1_fun/ppermute | solution.py:338
  42.2 6.6 %collective-permute-start.4 = (f32[32,128]{1,0:T(8,128)S(1)}, f32[32,128]{1,0:T(8,128)S(1)}, u32[]{:S(2)}, u32[]{:S(2)}) collective-permute-start(f32[32,128]{1,0:T(8,128)S(1)} %slice.23), channel_id=1, source_target_pairs={{0,2},{1,3},{2,0},{3,1},{4,6},{5,7},{6,4},{7,5},{8,10},{9,11},{10,... | collective-permute-start | bytes 49160 | tf_op jit(solution)/shard_map/cond/branch_1_fun/ppermute | solution.py:329
  48.8 1.7 %collective-permute-done.4 = f32[32,128]{1,0:T(8,128)S(1)} collective-permute-done((f32[32,128]{1,0:T(8,128)S(1)}, f32[32,128]{1,0:T(8,128)S(1)}, u32[]{:S(2)}, u32[]{:S(2)}) %collective-permute-start.4) | collective-permute-done | bytes 16416 | tf_op jit(solution)/shard_map/cond/branch_1_fun/ppermute | solution.py:329
  50.5 0.0 copy-start.3
  50.5 0.0 collective-permute-done.12
  50.5 0.8 %add.18 = f32[1024,128]{1,0:T(8,128)} add(f32[1024,128]{1,0:T(8,128)S(1)} %get-tuple-element.42, f32[1024,128]{1,0:T(8,128)S(1)} %collective-permute-done.12) | non-fusion elementwise | flops 131072 | bytes 1572864 | tf_op jit(solution)/shard_map/add | solution.py:375
  51.4 0.0 copy-done.3
  (9 shorter events, 0.1 us)
Async XLA Ops:
  0.6 6.7 %copy-start.4 = (f32[8,2,2,128]{3,2,1,0:T(2,128)S(1)}, f32[8,2,2,128]{3,2,1,0:T(2,128)}, u32[]{:S(2)}) copy-start(f32[8,2,2,128]{3,2,1,0:T(2,128)} %param.10) | copy-start | bytes 49156
  0.6 11.9 %copy-start = (f32[128,2,2,256]{3,2,1,0:T(2,128)S(1)}, f32[128,2,2,256]{3,2,1,0:T(2,128)}, u32[]{:S(2)}) copy-start(f32[128,2,2,256]{3,2,1,0:T(2,128)} %param.9) | copy-start | bytes 1572868
  1.9 10.5 %copy-start.5 = (s32[16]{0:T(128)S(1)}, s32[16]{0:T(128)}, u32[]{:S(2)}) copy-start(s32[16]{0:T(128)} %param.13) | copy-start | bytes 196
  1.9 10.5 %copy-start.6 = (s32[16]{0:T(128)S(1)}, s32[16]{0:T(128)}, u32[]{:S(2)}) copy-start(s32[16]{0:T(128)} %param.12) | copy-start | bytes 196
  1.9 13.6 %collective-permute-start.5 = (f32[512,128]{1,0:T(8,128)S(1)}, f32[512,128]{1,0:T(8,128)S(1)}, u32[]{:S(2)}, u32[]{:S(2)}) collective-permute-start(f32[512,128]{1,0:T(8,128)S(1)} %bitcast.19), channel_id=1, source_target_pairs={{1,0},{2,1},{3,2},{4,3},{5,4},{6,5},{7,6},{8,7},{9,8},{10,9},{11,1... | collective-permute-start | bytes 786440 | tf_op jit(solution)/shard_map/ppermute | solution.py:358
  7.4 8.1 %collective-permute-start.8 = (f32[32,128]{1,0:T(8,128)S(1)}, f32[32,128]{1,0:T(8,128)S(1)}, u32[]{:S(2)}, u32[]{:S(2)}) collective-permute-start(f32[32,128]{1,0:T(8,128)S(1)} %bitcast.21), channel_id=1, source_target_pairs={{0,12},{1,13},{2,14},{3,15},{4,8},{5,9},{6,10},{7,11},{8,4},{9,5},... | collective-permute-start | bytes 49160 | tf_op jit(solution)/shard_map/ppermute | solution.py:329
  7.8 7.6 %collective-permute-start.7 = (f32[32,128]{1,0:T(8,128)S(1)}, f32[32,128]{1,0:T(8,128)S(1)}, u32[]{:S(2)}, u32[]{:S(2)}) collective-permute-start(f32[32,128]{1,0:T(8,128)S(1)} %bitcast.22), channel_id=1, source_target_pairs={{0,4},{1,5},{2,6},{3,7},{4,0},{5,1},{6,2},{7,3},{8,12},{9,13},{10,... | collective-permute-start | bytes 49160 | tf_op jit(solution)/shard_map/ppermute | solution.py:329
  7.8 7.6 %collective-permute-start.6 = (f32[32,128]{1,0:T(8,128)S(1)}, f32[32,128]{1,0:T(8,128)S(1)}, u32[]{:S(2)}, u32[]{:S(2)}) collective-permute-start(f32[32,128]{1,0:T(8,128)S(1)} %bitcast.23), channel_id=1, source_target_pairs={{0,8},{1,9},{2,10},{3,11},{4,12},{5,13},{6,14},{7,15},{8,0},{9,1},... | collective-permute-start | bytes 49160 | tf_op jit(solution)/shard_map/ppermute | solution.py:329
  12.5 1.2 %copy-start.1 = (f32[16,128,128]{2,1,0:T(8,128)S(1)}, f32[16,128,128]{2,1,0:T(8,128)}, u32[]{:S(2)}) copy-start(f32[16,128,128]{2,1,0:T(8,128)} %patterns_ref.1) | copy-start | bytes 3145732
  13.7 1.1 %copy-start.2 = (f32[12,128,128]{2,1,0:T(8,128)S(1)}, f32[12,128,128]{2,1,0:T(8,128)}, u32[]{:S(2)}) copy-start(f32[12,128,128]{2,1,0:T(8,128)} %constant.7.clone.factors_ref) | copy-start | bytes 2359300
  15.5 4.3 %collective-permute-start.10 = (f32[128,128]{1,0:T(8,128)S(1)}, f32[128,128]{1,0:T(8,128)S(1)}, u32[]{:S(2)}, u32[]{:S(2)}) collective-permute-start(f32[128,128]{1,0:T(8,128)S(1)} %pad_maximum_fusion), channel_id=1, source_target_pairs={{0,2},{1,3},{2,0},{3,1},{4,6},{5,7},{6,4},{7,5},{8,10},{9,11},{10,... | collective-permute-start | bytes 196616 | tf_op jit(solution)/shard_map/ppermute | solution.py:329
  15.6 5.6 %collective-permute-start.9 = (f32[512,128]{1,0:T(8,128)S(1)}, f32[512,128]{1,0:T(8,128)S(1)}, u32[]{:S(2)}, u32[]{:S(2)}) collective-permute-start(f32[512,128]{1,0:T(8,128)S(1)} %bitcast.18), channel_id=1, source_target_pairs={{1,0},{2,1},{3,2},{4,3},{5,4},{6,5},{7,6},{8,7},{9,8},{10,9},{11,1... | collective-permute-start | bytes 786440 | tf_op jit(solution)/shard_map/ppermute | solution.py:364
  19.8 1.3 %collective-permute-start.11 = (f32[256,128]{1,0:T(8,128)S(1)}, f32[256,128]{1,0:T(8,128)S(1)}, u32[]{:S(2)}, u32[]{:S(2)}) collective-permute-start(f32[256,128]{1,0:T(8,128)S(1)} %constant_dynamic-update-slice_fusion.near_ref), channel_id=1, source_target_pairs={{0,1},{1,0},{2,3},{3,2},{4,5},{5,4},{6,7},{7,6},{8,9},{9,8},{10,11... | collective-permute-start | bytes 393224 | tf_op jit(solution)/shard_map/ppermute | solution.py:329
  31.9 18.6 %collective-permute-start.12 = (f32[1024,128]{1,0:T(8,128)S(1)}, f32[1024,128]{1,0:T(8,128)S(1)}, u32[]{:S(2)}, u32[]{:S(2)}) collective-permute-start(f32[1024,128]{1,0:T(8,128)S(1)} %get-tuple-element.43), channel_id=1, source_target_pairs={{0,1},{1,2},{2,3},{3,4},{4,5},{5,6},{6,7},{7,8},{8,9},{9,10},{10,1... | collective-permute-start | bytes 1572872 | tf_op jit(solution)/shard_map/ppermute | solution.py:369
  32.0 3.3 %collective-permute-start = (f32[256,128]{1,0:T(8,128)S(1)}, f32[256,128]{1,0:T(8,128)S(1)}, u32[]{:S(2)}, u32[]{:S(2)}) collective-permute-start(f32[256,128]{1,0:T(8,128)S(1)} %get-tuple-element.6), channel_id=1, source_target_pairs={{0,1},{1,0},{2,3},{3,2},{4,5},{5,4},{6,7},{7,6},{8,9},{9,8},{10,11... | collective-permute-start | bytes 393224 | tf_op jit(solution)/shard_map/cond/branch_1_fun/ppermute | solution.py:329
  35.4 5.0 %collective-permute-start.2 = (f32[64,128]{1,0:T(8,128)S(1)}, f32[64,128]{1,0:T(8,128)S(1)}, u32[]{:S(2)}, u32[]{:S(2)}) collective-permute-start(f32[64,128]{1,0:T(8,128)S(1)} %get-tuple-element.45), channel_id=1, source_target_pairs={{0,8},{1,9},{2,10},{3,11},{4,12},{5,13},{6,14},{7,15},{8,0},{9,1},... | collective-permute-start | bytes 98312 | tf_op jit(solution)/shard_map/cond/branch_1_fun/ppermute | solution.py:338
  35.5 4.9 %collective-permute-start.3 = (f32[64,128]{1,0:T(8,128)S(1)}, f32[64,128]{1,0:T(8,128)S(1)}, u32[]{:S(2)}, u32[]{:S(2)}) collective-permute-start(f32[64,128]{1,0:T(8,128)S(1)} %get-tuple-element.46), channel_id=1, source_target_pairs={{0,12},{1,13},{2,14},{3,15},{4,0},{5,1},{6,2},{7,3},{8,4},{9,5},{1... | collective-permute-start | bytes 98312 | tf_op jit(solution)/shard_map/cond/branch_1_fun/ppermute | solution.py:338
  35.6 6.6 %collective-permute-start.1 = (f32[64,128]{1,0:T(8,128)S(1)}, f32[64,128]{1,0:T(8,128)S(1)}, u32[]{:S(2)}, u32[]{:S(2)}) collective-permute-start(f32[64,128]{1,0:T(8,128)S(1)} %get-tuple-element.47), channel_id=1, source_target_pairs={{0,4},{1,5},{2,6},{3,7},{4,8},{5,9},{6,10},{7,11},{8,12},{9,13},{1... | collective-permute-start | bytes 98312 | tf_op jit(solution)/shard_map/cond/branch_1_fun/ppermute | solution.py:338
  42.2 8.4 %collective-permute-start.4 = (f32[32,128]{1,0:T(8,128)S(1)}, f32[32,128]{1,0:T(8,128)S(1)}, u32[]{:S(2)}, u32[]{:S(2)}) collective-permute-start(f32[32,128]{1,0:T(8,128)S(1)} %slice.23), channel_id=1, source_target_pairs={{0,2},{1,3},{2,0},{3,1},{4,6},{5,7},{6,4},{7,5},{8,10},{9,11},{10,... | collective-permute-start | bytes 49160 | tf_op jit(solution)/shard_map/cond/branch_1_fun/ppermute | solution.py:329
  50.5 0.9 %copy-start.3 = (f32[8,2,2,128]{3,2,1,0:T(2,128)}, f32[8,2,2,128]{3,2,1,0:T(2,128)S(1)}, u32[]{:S(2)}) copy-start(f32[8,2,2,128]{3,2,1,0:T(2,128)S(1)} %get-tuple-element.50) | copy-start | bytes 49156

commit v4 on v3

--- a/solution.py
+++ b/solution.py
@@ -37,15 +37,10 @@
     return high, low
 
 
-def prepare(own_ref, patterns_ref, factors_ref, planes_out, patterns_out, mats_out, half_out, own, parts, sems):
-    copies = [pltpu.make_async_copy(source, target, sems.at[i]) for i, (source, target) in enumerate(
-        ((factors_ref, parts), (own_ref, own), (patterns_ref, patterns_out)))]
-    for copy in copies:
-        copy.start()
-    copies[0].wait()
-    extent = parts.shape[1]
+def matrices(factors_ref, mats_out, half_out):
+    extent = factors_ref.shape[1]
     for kind in range(2):
-        real, imag = split(parts[2 * kind]), split(parts[2 * kind + 1])
+        real, imag = split(factors_ref[2 * kind]), split(factors_ref[2 * kind + 1])
         for conj in range(2):
             for k in range(2):
                 mat = 4 * kind + 2 * conj + k
@@ -55,12 +50,19 @@
                 mats_out[mat, extent:, :extent] = lower
                 mats_out[mat, extent:, extent:] = real[k]
     for k in range(half_out.shape[0]):
-        high, low = split(parts[4 + k])
+        high, low = split(factors_ref[4 + k])
         half_out[k, :extent, :extent] = high
         half_out[k, :extent, extent:] = high
         half_out[k, extent:, :extent] = low
         half_out[k, extent:, extent:] = low
-    copies[1].wait()
+
+
+def prepare(own_ref, patterns_ref, planes_out, patterns_out, own, sems):
+    copies = [pltpu.make_async_copy(source, target, sems.at[i]) for i, (source, target) in enumerate(
+        ((own_ref, own), (patterns_ref, patterns_out)))]
+    for copy in copies:
+        copy.start()
+    copies[0].wait()
     rows = planes_out.shape[1]
     for layer in range(SLICES):
         for half in range(HALVES):
@@ -68,7 +70,7 @@
                 source = (layer * HALVES + half) * 2 + part
                 plane = (layer * 2 + part) * HALVES + half
                 planes_out[plane] = own[pl.ds(source, rows, stride=8), :]
-    copies[2].wait()
+    copies[1].wait()
 
 
 def times(a, b):
@@ -257,27 +259,31 @@
 
 
 def prepared(own, patterns):
-    extent = patterns.shape[1]
     vmem = pl.BlockSpec(memory_space=pltpu.VMEM)
-    parts = jnp.asarray(factors(extent))
     return pl.pallas_call(
         prepare,
         out_shape=(
             jax.ShapeDtypeStruct((8, own.shape[0] // 8, own.shape[1]), jnp.float32),
             jax.ShapeDtypeStruct(patterns.shape, jnp.float32),
-            jax.ShapeDtypeStruct((8, 2 * extent, 2 * extent), jnp.bfloat16),
-            jax.ShapeDtypeStruct((8, 2 * extent, 2 * extent), jnp.bfloat16),
         ),
-        in_specs=[pl.BlockSpec(memory_space=pltpu.HBM)] * 3,
-        out_specs=(vmem,) * 4,
-        scratch_shapes=[
-            pltpu.VMEM(own.shape, jnp.float32),
-            pltpu.VMEM(parts.shape, jnp.float32),
-            pltpu.SemaphoreType.DMA((3,)),
-        ],
+        in_specs=[pl.BlockSpec(memory_space=pltpu.HBM)] * 2,
+        out_specs=(vmem,) * 2,
+        scratch_shapes=[pltpu.VMEM(own.shape, jnp.float32), pltpu.SemaphoreType.DMA((2,))],
         compiler_params=pltpu.CompilerParams(vmem_limit_bytes=16 * 1024 * 1024),
-        cost_estimate=pl.CostEstimate(flops=0, bytes_accessed=6 * 1024 * 1024, transcendentals=0),
-    )(own, patterns, parts)
+        cost_estimate=pl.CostEstimate(flops=0, bytes_accessed=4 * 1024 * 1024, transcendentals=0),
+    )(own, patterns)
+
+
+def built_matrices(extent):
+    vmem = pl.BlockSpec(memory_space=pltpu.VMEM)
+    return pl.pallas_call(
+        matrices,
+        out_shape=(jax.ShapeDtypeStruct((8, 2 * extent, 2 * extent), jnp.bfloat16),) * 2,
+        in_specs=[vmem],
+        out_specs=(vmem,) * 2,
+        compiler_params=pltpu.CompilerParams(vmem_limit_bytes=16 * 1024 * 1024),
+        cost_estimate=pl.CostEstimate(flops=0, bytes_accessed=3 * 1024 * 1024, transcendentals=0),
+    )(jnp.asarray(factors(extent)))
 
 
 def terms(scalars, planes, low, high, near, far, patterns, mats):
@@ -357,11 +363,12 @@
     low, high, mine = lax.optimization_barrier((low, high, flat(probe_field)))
     low = lax.ppermute(low, "tile", down)
     quarter = jnp.concatenate([mine, partner(mine, 8), partner(mine, 4), partner(mine, 12)], axis=0)
-    planes, patterns, *mats = prepared(own, patterns)
-    low, high, quarter, planes, patterns, scalars, *mats = lax.optimization_barrier(
-        (low, high, quarter, planes, patterns, scalars, *mats))
+    mats = built_matrices(patterns.shape[1])
+    low, high, quarter, patterns, own, *mats = lax.optimization_barrier((low, high, quarter, patterns, own, *mats))
     near = jnp.concatenate([quarter, partner(quarter, 2)], axis=0)
     high = lax.ppermute(high, "tile", down)
+    planes, patterns = prepared(own, patterns)
+    near, planes, patterns, scalars = lax.optimization_barrier((near, planes, patterns, scalars))
     far = partner(near, 1)
 
     own_grad, back, probe_grad = terms(scalars, planes, low, high, near, far, patterns, mats)

time: 52.1 us -> 53.1 us (1.019)
  starting transfers between devices: 21.5 us -> 32.5 us
  Pallas kernels: 11.3 us -> 4.54 us
  waiting for transfers between devices: 12.5 us -> 9.88 us
  local copies, waits for them, and re-layouts: 3.63 us -> 2.83 us
    pallas_call x1, Pallas kernels: 10.7 us -> 4.01 us  [terms(): pl.pallas_call(kernel, out_shape=(jax.ShapeDtypeStruct((planes.shape[1] *...]
    ppermute x1, starting transfers between devices: 0.06 us -> 5.57 us  [shards(): lax.ppermute(back, 'tile', [(i, (i + 1) % size) for i in range(size)])]
    ppermute x3, starting transfers between devices: 2.16 us -> 5.18 us  [places_on(): lax.ppermute(value, 'tile', [(i, i // GROUP_DEV * GROUP_DEV + (i + distan...]
    ppermute x7, waiting for transfers between devices: 7.92 us -> 5.63 us  [partner(): lax.ppermute(value, 'tile', [(i, i ^ bits) for i in range(lax.axis_size('...]
    ppermute x1, starting transfers between devices: 0.38 us -> 2.35 us  [shards(): high = lax.ppermute(high, 'tile', down)]
    ppermute x3, waiting for transfers between devices: 4.53 us -> 3.69 us  [places_on(): lax.ppermute(value, 'tile', [(i, i // GROUP_DEV * GROUP_DEV + (i + distan...]
    unnamed x15 -> x14, local copies, waits for them, and re-layouts: 2.39 us -> 1.57 us
    ppermute x1, waiting for transfers between devices: 0.01 us -> 0.56 us  [shards(): high = lax.ppermute(high, 'tile', down)]
  transfers between devices with their start and end apart: 13 -> 13, of which waited for: 6 -> 8; matrix products, arithmetic and copies ran while one was open for 0% -> 0% of each run, Pallas kernels for 1% -> 1%
where the time goes in v4:
time: 53.1 us; the launch traced here: 52.2 us
  starting transfers between devices  32.5 us (61%)
  waiting for transfers between devices  9.88 us (19%)
  Pallas kernels  4.54 us (9%)
  local copies, waits for them, and re-layouts  2.83 us (5%)
  between operations  1.4 us (3%)
  other arithmetic  0.97 us (2%)
    ppermute x7, starting transfers between devices, partner(): lax.ppermute(value, 'tile', [(i, i ^ bits) for i in range(lax.axis_size('...  13.9 us
    ppermute x7, waiting for transfers between devices, partner(): lax.ppermute(value, 'tile', [(i, i ^ bits) for i in range(lax.axis_size('...  5.63 us
    ppermute x1, starting transfers between devices, shards(): lax.ppermute(back, 'tile', [(i, (i + 1) % size) for i in range(size)])  5.57 us
    ppermute x1, starting transfers between devices, shards(): low = lax.ppermute(low, 'tile', down)  5.47 us
    ppermute x3, starting transfers between devices, places_on(): lax.ppermute(value, 'tile', [(i, i // GROUP_DEV * GROUP_DEV + (i + distan...  5.18 us
    pallas_call x1, Pallas kernels, terms(): pl.pallas_call(kernel, out_shape=(jax.ShapeDtypeStruct((planes.shape[1] *...  4.01 us
    ppermute x3, waiting for transfers between devices, places_on(): lax.ppermute(value, 'tile', [(i, i // GROUP_DEV * GROUP_DEV + (i + distan...  3.69 us
    ppermute x1, starting transfers between devices, shards(): high = lax.ppermute(high, 'tile', down)  2.35 us
  transfers between devices with their start and end apart: 13, of which 8 were waited for; matrix products, arithmetic and copies ran while one was open for 0% of the time, Pallas kernels for 1%

profile of v4, /device:TPU:0, one launch (start us, length us, event | category | flops | bytes accessed | tf_op | source)
XLA Modules:
  0.0 52.2 jit_solution(836394481969839399)
XLA Ops:
  0.6 0.0 copy-start.1
  0.6 1.3 %fusion.1 = (f32[64,2,2,2,128]{4,3,2,1,0:T(2,128)S(1)}, f32[64,2,2,2,128]{4,3,2,1,0:T(2,128)S(1)}) fusion(f32[128,2,2,2,128]{4,3,2,1,0:T(2,128)} %bitcast.15), kind=kLoop, calls=%fused_computation.6 | loop fusion | bytes 1048576 | tf_op jit(solution)/shard_map/slice | solution.py:339
  1.9 0.0 copy-start
  1.9 5.5 %collective-permute-start.5 = (f32[512,128]{1,0:T(8,128)S(1)}, f32[512,128]{1,0:T(8,128)S(1)}, u32[]{:S(2)}, u32[]{:S(2)}) collective-permute-start(f32[512,128]{1,0:T(8,128)S(1)} %bitcast.19), channel_id=1, source_target_pairs={{1,0},{2,1},{3,2},{4,3},{5,4},{6,5},{7,6},{8,7},{9,8},{10,9},{11,1... | collective-permute-start | bytes 786440 | tf_op jit(solution)/shard_map/ppermute | solution.py:364
  7.4 0.4 collective-permute-start.8
  7.8 0.0 collective-permute-start.7
  7.8 3.9 %collective-permute-start.6 = (f32[32,128]{1,0:T(8,128)}, f32[32,128]{1,0:T(8,128)S(1)}, u32[]{:S(2)}, u32[]{:S(2)}) collective-permute-start(f32[32,128]{1,0:T(8,128)} %bitcast.23), channel_id=1, source_target_pairs={{0,8},{1,9},{2,10},{3,11},{4,12},{5,13},{6,14},{7,15},{8,0},{9,1},... | collective-permute-start | bytes 49160 | tf_op jit(solution)/shard_map/ppermute | solution.py:335
  12.4 0.0 copy-start.2
  12.4 1.1 %copy-done.2 = f32[12,128,128]{2,1,0:T(8,128)S(1)} copy-done((f32[12,128,128]{2,1,0:T(8,128)S(1)}, f32[12,128,128]{2,1,0:T(8,128)}, u32[]{:S(2)}) %copy-start.2) | copy-done | bytes 786456
  13.6 0.0 copy-start.4
  13.6 0.3 shard_map.86
  13.8 0.0 collective-permute-done.8
  13.8 0.0 collective-permute-done.7
  13.9 0.0 collective-permute-done.6
  13.9 0.4 copy-done.4
  14.3 0.0 collective-permute-done.5.low_ref
  14.3 0.0 copy-start.5
  14.3 0.0 copy-start.6
  14.3 0.1 collective-permute-start.9
  14.4 2.3 %collective-permute-start.10 = (f32[512,128]{1,0:T(8,128)S(1)}, f32[512,128]{1,0:T(8,128)S(1)}, u32[]{:S(2)}, u32[]{:S(2)}) collective-permute-start(f32[512,128]{1,0:T(8,128)S(1)} %bitcast.18), channel_id=1, source_target_pairs={{1,0},{2,1},{3,2},{4,3},{5,4},{6,5},{7,6},{8,7},{9,8},{10,9},{11,1... | collective-permute-start | bytes 786440 | tf_op jit(solution)/shard_map/ppermute | solution.py:369
  16.7 0.0 copy-done.5
  16.7 0.0 copy-done.6
  16.7 0.1 pad_add_fusion.scalars_ref
  16.8 0.0 copy-done.1
  16.8 0.0 copy-done
  16.8 0.2 shard_map.87
  17.1 1.6 %collective-permute-done.9 = f32[128,128]{1,0:T(8,128)S(1)} collective-permute-done((f32[128,128]{1,0:T(8,128)S(1)}, f32[128,128]{1,0:T(8,128)S(1)}, u32[]{:S(2)}, u32[]{:S(2)}) %collective-permute-start.9) | collective-permute-done | bytes 65568 | tf_op jit(solution)/shard_map/ppermute | solution.py:335
  18.7 0.1 collective-permute-start.11
  18.7 1.3 %collective-permute-done.11.far_ref = f32[256,128]{1,0:T(8,128)S(1)} collective-permute-done((f32[256,128]{1,0:T(8,128)S(1)}, f32[256,128]{1,0:T(8,128)S(1)}, u32[]{:S(2)}, u32[]{:S(2)}) %collective-permute-start.11) | collective-permute-done | bytes 131104 | tf_op jit(solution)/shard_map/ppermute | solution.py:335
  20.1 0.6 %collective-permute-done.10.high_ref = f32[512,128]{1,0:T(8,128)S(1)} collective-permute-done((f32[512,128]{1,0:T(8,128)S(1)}, f32[512,128]{1,0:T(8,128)S(1)}, u32[]{:S(2)}, u32[]{:S(2)}) %collective-permute-start.10) | collective-permute-done | bytes 262176 | tf_op jit(solution)/shard_map/ppermute | solution.py:369
  20.6 4.0 %shard_map.88 = (f32[1024,128]{1,0:T(8,128)S(1)}, f32[1024,128]{1,0:T(8,128)S(1)}, f32[4,128,128]{2,1,0:T(8,128)S(1)}) custom-call(s32[33]{0:T(128)S(1)} %pad_add_fusion.scalars_ref, f32[8,128,128]{2,1,0:T(8,128)S(1)} %get-tuple-element.41.own_ref, f32[512,128]{1,0:T(8,128)S(1)} %collective-permute-done.5.low_ref, ...), custom_call_target="tpu_custom_call" | custom-call | tf_op jit(solution)/shard_map/pallas_call | solution.py:294
  24.6 5.6 %collective-permute-start.12 = (f32[1024,128]{1,0:T(8,128)S(1)}, f32[1024,128]{1,0:T(8,128)S(1)}, u32[]{:S(2)}, u32[]{:S(2)}) collective-permute-start(f32[1024,128]{1,0:T(8,128)S(1)} %get-tuple-element.49), channel_id=1, source_target_pairs={{0,1},{1,2},{2,3},{3,4},{4,5},{5,6},{6,7},{7,8},{8,9},{9,10},{10,1... | collective-permute-start | bytes 1572872 | tf_op jit(solution)/shard_map/ppermute | solution.py:376
  30.2 21.1 %conditional.1 = (f32[8,2,2,128]{3,2,1,0:T(2,128)S(1)}) conditional(s32[]{:T(128)} %bitcast.11, () %tuple.22, f32[4,128,128]{2,1,0:T(8,128)S(1)} %get-tuple-element.50), branch_computations={%region_0.0_spmd, %region_1.0_spmd} | conditional | flops 61440 | bytes 1818832 | solution.py:377
  30.3 1.7 %collective-permute-start = (f32[256,128]{1,0:T(8,128)S(1)}, f32[256,128]{1,0:T(8,128)S(1)}, u32[]{:S(2)}, u32[]{:S(2)}) collective-permute-start(f32[256,128]{1,0:T(8,128)S(1)} %get-tuple-element.6), channel_id=1, source_target_pairs={{0,1},{1,0},{2,3},{3,2},{4,5},{5,4},{6,7},{7,6},{8,9},{9,8},{10,11... | collective-permute-start | bytes 393224 | tf_op jit(solution)/shard_map/cond/branch_1_fun/ppermute | solution.py:335
  32.0 1.0 %collective-permute-done = f32[256,128]{1,0:T(8,128)S(1)} collective-permute-done((f32[256,128]{1,0:T(8,128)S(1)}, f32[256,128]{1,0:T(8,128)S(1)}, u32[]{:S(2)}, u32[]{:S(2)}) %collective-permute-start) | collective-permute-done | bytes 131104 | tf_op jit(solution)/shard_map/cond/branch_1_fun/ppermute | solution.py:335
  33.0 3.2 %collective-permute-start.2 = (f32[64,128]{1,0:T(8,128)S(1)}, f32[64,128]{1,0:T(8,128)S(1)}, u32[]{:S(2)}, u32[]{:S(2)}) collective-permute-start(f32[64,128]{1,0:T(8,128)S(1)} %get-tuple-element.51), channel_id=1, source_target_pairs={{0,8},{1,9},{2,10},{3,11},{4,12},{5,13},{6,14},{7,15},{8,0},{9,1},... | collective-permute-start | bytes 98312 | tf_op jit(solution)/shard_map/cond/branch_1_fun/ppermute | solution.py:344
  36.2 0.0 collective-permute-start.3
  36.2 2.0 %collective-permute-start.1 = (f32[64,128]{1,0:T(8,128)S(1)}, f32[64,128]{1,0:T(8,128)S(1)}, u32[]{:S(2)}, u32[]{:S(2)}) collective-permute-start(f32[64,128]{1,0:T(8,128)S(1)} %get-tuple-element.53), channel_id=1, source_target_pairs={{0,4},{1,5},{2,6},{3,7},{4,8},{5,9},{6,10},{7,11},{8,12},{9,13},{1... | collective-permute-start | bytes 98312 | tf_op jit(solution)/shard_map/cond/branch_1_fun/ppermute | solution.py:344
  38.2 0.2 collective-permute-done.2
  38.4 1.7 %collective-permute-done.3 = f32[64,128]{1,0:T(8,128)S(1)} collective-permute-done((f32[64,128]{1,0:T(8,128)S(1)}, f32[64,128]{1,0:T(8,128)S(1)}, u32[]{:S(2)}, u32[]{:S(2)}) %collective-permute-start.3) | collective-permute-done | bytes 32800 | tf_op jit(solution)/shard_map/cond/branch_1_fun/ppermute | solution.py:344
  40.1 1.8 %collective-permute-done.1 = f32[64,128]{1,0:T(8,128)S(1)} collective-permute-done((f32[64,128]{1,0:T(8,128)S(1)}, f32[64,128]{1,0:T(8,128)S(1)}, u32[]{:S(2)}, u32[]{:S(2)}) %collective-permute-start.1) | collective-permute-done | bytes 32800 | tf_op jit(solution)/shard_map/cond/branch_1_fun/ppermute | solution.py:344
  41.9 7.7 %collective-permute-start.4 = (f32[32,128]{1,0:T(8,128)S(1)}, f32[32,128]{1,0:T(8,128)S(1)}, u32[]{:S(2)}, u32[]{:S(2)}) collective-permute-start(f32[32,128]{1,0:T(8,128)S(1)} %slice.23), channel_id=1, source_target_pairs={{0,2},{1,3},{2,0},{3,1},{4,6},{5,7},{6,4},{7,5},{8,10},{9,11},{10,... | collective-permute-start | bytes 49160 | tf_op jit(solution)/shard_map/cond/branch_1_fun/ppermute | solution.py:335
  49.6 1.7 %collective-permute-done.4 = f32[32,128]{1,0:T(8,128)S(1)} collective-permute-done((f32[32,128]{1,0:T(8,128)S(1)}, f32[32,128]{1,0:T(8,128)S(1)}, u32[]{:S(2)}, u32[]{:S(2)}) %collective-permute-start.4) | collective-permute-done | bytes 16416 | tf_op jit(solution)/shard_map/cond/branch_1_fun/ppermute | solution.py:335
  51.3 0.0 copy-start.3
  51.3 0.0 collective-permute-done.12
  51.3 0.8 %add.18 = f32[1024,128]{1,0:T(8,128)} add(f32[1024,128]{1,0:T(8,128)S(1)} %get-tuple-element.48, f32[1024,128]{1,0:T(8,128)S(1)} %collective-permute-done.12) | non-fusion elementwise | flops 131072 | bytes 1572864 | tf_op jit(solution)/shard_map/add | solution.py:382
  52.2 0.0 copy-done.3
  (8 shorter events, 0.1 us)
Async XLA Ops:
  0.6 16.2 %copy-start.1 = (f32[16,128,128]{2,1,0:T(8,128)S(1)}, f32[16,128,128]{2,1,0:T(8,128)}, u32[]{:S(2)}) copy-start(f32[16,128,128]{2,1,0:T(8,128)} %patterns_ref) | copy-start | bytes 3145732
  1.9 14.9 %copy-start = (f32[128,2,2,256]{3,2,1,0:T(2,128)S(1)}, f32[128,2,2,256]{3,2,1,0:T(2,128)}, u32[]{:S(2)}) copy-start(f32[128,2,2,256]{3,2,1,0:T(2,128)} %param.9) | copy-start | bytes 1572868
  1.9 12.4 %collective-permute-start.5 = (f32[512,128]{1,0:T(8,128)S(1)}, f32[512,128]{1,0:T(8,128)S(1)}, u32[]{:S(2)}, u32[]{:S(2)}) collective-permute-start(f32[512,128]{1,0:T(8,128)S(1)} %bitcast.19), channel_id=1, source_target_pairs={{1,0},{2,1},{3,2},{4,3},{5,4},{6,5},{7,6},{8,7},{9,8},{10,9},{11,1... | collective-permute-start | bytes 786440 | tf_op jit(solution)/shard_map/ppermute | solution.py:364
  7.4 6.5 %collective-permute-start.8 = (f32[32,128]{1,0:T(8,128)}, f32[32,128]{1,0:T(8,128)S(1)}, u32[]{:S(2)}, u32[]{:S(2)}) collective-permute-start(f32[32,128]{1,0:T(8,128)} %bitcast.21), channel_id=1, source_target_pairs={{0,12},{1,13},{2,14},{3,15},{4,8},{5,9},{6,10},{7,11},{8,4},{9,5},... | collective-permute-start | bytes 49160 | tf_op jit(solution)/shard_map/ppermute | solution.py:335
  7.8 6.0 %collective-permute-start.7 = (f32[32,128]{1,0:T(8,128)}, f32[32,128]{1,0:T(8,128)S(1)}, u32[]{:S(2)}, u32[]{:S(2)}) collective-permute-start(f32[32,128]{1,0:T(8,128)} %bitcast.22), channel_id=1, source_target_pairs={{0,4},{1,5},{2,6},{3,7},{4,0},{5,1},{6,2},{7,3},{8,12},{9,13},{10,... | collective-permute-start | bytes 49160 | tf_op jit(solution)/shard_map/ppermute | solution.py:335
  7.8 6.0 %collective-permute-start.6 = (f32[32,128]{1,0:T(8,128)}, f32[32,128]{1,0:T(8,128)S(1)}, u32[]{:S(2)}, u32[]{:S(2)}) collective-permute-start(f32[32,128]{1,0:T(8,128)} %bitcast.23), channel_id=1, source_target_pairs={{0,8},{1,9},{2,10},{3,11},{4,12},{5,13},{6,14},{7,15},{8,0},{9,1},... | collective-permute-start | bytes 49160 | tf_op jit(solution)/shard_map/ppermute | solution.py:335
  12.4 1.1 %copy-start.2 = (f32[12,128,128]{2,1,0:T(8,128)S(1)}, f32[12,128,128]{2,1,0:T(8,128)}, u32[]{:S(2)}) copy-start(f32[12,128,128]{2,1,0:T(8,128)} %constant.7.clone.factors_ref) | copy-start | bytes 2359300
  13.6 0.7 %copy-start.4 = (f32[8,2,2,128]{3,2,1,0:T(2,128)S(1)}, f32[8,2,2,128]{3,2,1,0:T(2,128)}, u32[]{:S(2)}) copy-start(f32[8,2,2,128]{3,2,1,0:T(2,128)} %param.10) | copy-start | bytes 49156
  14.3 2.5 %copy-start.5 = (s32[16]{0:T(128)S(1)}, s32[16]{0:T(128)}, u32[]{:S(2)}) copy-start(s32[16]{0:T(128)} %param.13) | copy-start | bytes 196
  14.3 2.4 %copy-start.6 = (s32[16]{0:T(128)S(1)}, s32[16]{0:T(128)}, u32[]{:S(2)}) copy-start(s32[16]{0:T(128)} %param.12) | copy-start | bytes 196
  14.3 4.3 %collective-permute-start.9 = (f32[128,128]{1,0:T(8,128)S(1)}, f32[128,128]{1,0:T(8,128)S(1)}, u32[]{:S(2)}, u32[]{:S(2)}) collective-permute-start(f32[128,128]{1,0:T(8,128)S(1)} %pad_maximum_fusion.1), channel_id=1, source_target_pairs={{0,2},{1,3},{2,0},{3,1},{4,6},{5,7},{6,4},{7,5},{8,10},{9,11},{10,... | collective-permute-start | bytes 196616 | tf_op jit(solution)/shard_map/ppermute | solution.py:335
  14.4 6.2 %collective-permute-start.10 = (f32[512,128]{1,0:T(8,128)S(1)}, f32[512,128]{1,0:T(8,128)S(1)}, u32[]{:S(2)}, u32[]{:S(2)}) collective-permute-start(f32[512,128]{1,0:T(8,128)S(1)} %bitcast.18), channel_id=1, source_target_pairs={{1,0},{2,1},{3,2},{4,3},{5,4},{6,5},{7,6},{8,7},{9,8},{10,9},{11,1... | collective-permute-start | bytes 786440 | tf_op jit(solution)/shard_map/ppermute | solution.py:369
  18.7 1.4 %collective-permute-start.11 = (f32[256,128]{1,0:T(8,128)S(1)}, f32[256,128]{1,0:T(8,128)S(1)}, u32[]{:S(2)}, u32[]{:S(2)}) collective-permute-start(f32[256,128]{1,0:T(8,128)S(1)} %pad_maximum_fusion.near_ref), channel_id=1, source_target_pairs={{0,1},{1,0},{2,3},{3,2},{4,5},{5,4},{6,7},{7,6},{8,9},{9,8},{10,11... | collective-permute-start | bytes 393224 | tf_op jit(solution)/shard_map/ppermute | solution.py:335
  24.6 26.7 %collective-permute-start.12 = (f32[1024,128]{1,0:T(8,128)S(1)}, f32[1024,128]{1,0:T(8,128)S(1)}, u32[]{:S(2)}, u32[]{:S(2)}) collective-permute-start(f32[1024,128]{1,0:T(8,128)S(1)} %get-tuple-element.49), channel_id=1, source_target_pairs={{0,1},{1,2},{2,3},{3,4},{4,5},{5,6},{6,7},{7,8},{8,9},{9,10},{10,1... | collective-permute-start | bytes 1572872 | tf_op jit(solution)/shard_map/ppermute | solution.py:376
  30.3 2.7 %collective-permute-start = (f32[256,128]{1,0:T(8,128)S(1)}, f32[256,128]{1,0:T(8,128)S(1)}, u32[]{:S(2)}, u32[]{:S(2)}) collective-permute-start(f32[256,128]{1,0:T(8,128)S(1)} %get-tuple-element.6), channel_id=1, source_target_pairs={{0,1},{1,0},{2,3},{3,2},{4,5},{5,4},{6,7},{7,6},{8,9},{9,8},{10,11... | collective-permute-start | bytes 393224 | tf_op jit(solution)/shard_map/cond/branch_1_fun/ppermute | solution.py:335
  33.0 5.4 %collective-permute-start.2 = (f32[64,128]{1,0:T(8,128)S(1)}, f32[64,128]{1,0:T(8,128)S(1)}, u32[]{:S(2)}, u32[]{:S(2)}) collective-permute-start(f32[64,128]{1,0:T(8,128)S(1)} %get-tuple-element.51), channel_id=1, source_target_pairs={{0,8},{1,9},{2,10},{3,11},{4,12},{5,13},{6,14},{7,15},{8,0},{9,1},... | collective-permute-start | bytes 98312 | tf_op jit(solution)/shard_map/cond/branch_1_fun/ppermute | solution.py:344
  36.2 3.9 %collective-permute-start.3 = (f32[64,128]{1,0:T(8,128)S(1)}, f32[64,128]{1,0:T(8,128)S(1)}, u32[]{:S(2)}, u32[]{:S(2)}) collective-permute-start(f32[64,128]{1,0:T(8,128)S(1)} %get-tuple-element.52), channel_id=1, source_target_pairs={{0,12},{1,13},{2,14},{3,15},{4,0},{5,1},{6,2},{7,3},{8,4},{9,5},{1... | collective-permute-start | bytes 98312 | tf_op jit(solution)/shard_map/cond/branch_1_fun/ppermute | solution.py:344
  36.2 5.7 %collective-permute-start.1 = (f32[64,128]{1,0:T(8,128)S(1)}, f32[64,128]{1,0:T(8,128)S(1)}, u32[]{:S(2)}, u32[]{:S(2)}) collective-permute-start(f32[64,128]{1,0:T(8,128)S(1)} %get-tuple-element.53), channel_id=1, source_target_pairs={{0,4},{1,5},{2,6},{3,7},{4,8},{5,9},{6,10},{7,11},{8,12},{9,13},{1... | collective-permute-start | bytes 98312 | tf_op jit(solution)/shard_map/cond/branch_1_fun/ppermute | solution.py:344
  41.9 9.4 %collective-permute-start.4 = (f32[32,128]{1,0:T(8,128)S(1)}, f32[32,128]{1,0:T(8,128)S(1)}, u32[]{:S(2)}, u32[]{:S(2)}) collective-permute-start(f32[32,128]{1,0:T(8,128)S(1)} %slice.23), channel_id=1, source_target_pairs={{0,2},{1,3},{2,0},{3,1},{4,6},{5,7},{6,4},{7,5},{8,10},{9,11},{10,... | collective-permute-start | bytes 49160 | tf_op jit(solution)/shard_map/cond/branch_1_fun/ppermute | solution.py:335
  51.3 0.9 %copy-start.3 = (f32[8,2,2,128]{3,2,1,0:T(2,128)}, f32[8,2,2,128]{3,2,1,0:T(2,128)S(1)}, u32[]{:S(2)}) copy-start(f32[8,2,2,128]{3,2,1,0:T(2,128)S(1)} %get-tuple-element.56) | copy-start | bytes 49156
